TPU v7x, 32 devices: a whole 2x2x4 slice. The times are simulated.
32 devices in a mesh: section: 2 (over x), dp: 16 (over z, y, core).
Axes of the slice: x: 2, y: 2, z: 4, core: 2. Of those that a mesh axis runs over, the one named last changes fastest.
Arguments:
- tokens: bfloat16 [7680, 1024], P('dp'), may hold values from -6 to 6
- cotangent: bfloat16 [7680, 1024], P('dp'), may hold values from -6 to 6
- norm_gains: float32 [2, 2, 1024], P('section'), may hold values from 0.1 to 1.9
- norm_biases: float32 [2, 2, 1024], P('section'), may hold values from -3 to 3
- w_qkv: bfloat16 [2, 1024, 3072], P('section'), may hold values from -0.1875 to 0.1875
- w_out: bfloat16 [2, 1024, 1024], P('section'), may hold values from -0.375 to 0.375
- w_up: bfloat16 [2, 1024, 2048], P('section'), may hold values from -0.1875 to 0.1875
- w_down: bfloat16 [2, 2048, 1024], P('section'), may hold values from -0.125 to 0.125
Outputs:
- mixed: bfloat16 [2, 7680, 1024], P('section', 'dp')
- grad_inputs: bfloat16 [2, 7680, 1024], P('section', 'dp')
- grad_qkv: float32 [2, 1024, 3072], P('section', 'dp')
- grad_out: float32 [2, 1024, 1024], P('section', None, 'dp')
- grad_up: float32 [2, 1024, 2048], P('section', 'dp')
- grad_down: float32 [2, 2048, 1024], P('section', None, 'dp')
- grad_gains: float32 [2, 2, 1024], P('section', None, 'dp')
- grad_biases: float32 [2, 2, 1024], P('section', None, 'dp')
All inputs are finite; a program needn't handle non-finite values.
Results may differ from a plain program's by a relative error of at most 0.015.
Values may be sent and summed in bfloat16 or wider, within the bound.
A program may use at most 256 MiB of HBM per device.

v0:
```python
import math

import jax
import jax.numpy as jnp
from jax import lax
from jax.sharding import PartitionSpec as P

HEADS = 8
HEAD_DIM = 128
ITEM_LEN = 15
MICRO = 4


EPSILON = 1e-05


def passed_along(block, axis, distance):
    devices = range(lax.axis_size(axis))
    route = [(i - distance, i) for i in devices if i - distance in devices]
    return lax.ppermute(block, axis, route)


def normalize(values, gain, offset):
    average = jnp.mean(values, axis=-1, keepdims=True)
    centered = values - average
    variance = jnp.mean(centered * centered, axis=-1, keepdims=True)
    return centered * lax.rsqrt(variance + EPSILON) * gain + offset


def gelu_tanh(u):
    return 0.5 * u * (1.0 + jnp.tanh(0.7978845608 * (u + 0.044715 * u * u * u)))


def item_mask(row_count):
    row_ids = lax.broadcasted_iota(jnp.int32, (row_count, row_count), 0)
    col_ids = lax.broadcasted_iota(jnp.int32, (row_count, row_count), 1)
    return (row_ids // ITEM_LEN == col_ids // ITEM_LEN) & (col_ids <= row_ids)


def forward(inputs, weights):
    gains, biases, w_qkv, w_out, w_up, w_down = weights
    row_count = inputs.shape[0]
    hidden = inputs.astype(jnp.float32)
    normed = normalize(hidden, gains[0], biases[0]).astype(jnp.bfloat16)
    project = jnp.dot(normed, w_qkv, preferred_element_type=jnp.float32).astype(jnp.bfloat16)
    shaped = project.reshape(row_count, 3, HEADS, HEAD_DIM)
    scale = 1.0 / math.sqrt(HEAD_DIM)
    scores = (
        jnp.einsum("rhd,chd->hrc", shaped[:, 0], shaped[:, 1], preferred_element_type=jnp.float32)
        * scale
    )
    scores = jnp.where(item_mask(row_count), scores, -1e30)
    row_max = jnp.max(scores, axis=-1, keepdims=True)
    exponent = jnp.exp(scores - row_max)
    probs = exponent / jnp.sum(exponent, axis=-1, keepdims=True)
    context = jnp.einsum(
        "hrc,chd->rhd", probs.astype(jnp.bfloat16), shaped[:, 2], preferred_element_type=jnp.float32
    )
    context = context.reshape(row_count, HEADS * HEAD_DIM).astype(jnp.bfloat16)
    middle = hidden + jnp.dot(context, w_out, preferred_element_type=jnp.float32)
    normed_two = normalize(middle, gains[1], biases[1]).astype(jnp.bfloat16)
    upward = jnp.dot(normed_two, w_up, preferred_element_type=jnp.float32)
    active = gelu_tanh(upward).astype(jnp.bfloat16)
    output = (middle + jnp.dot(active, w_down, preferred_element_type=jnp.float32)).astype(
        jnp.bfloat16
    )
    return (output, (hidden, normed, project, probs, context, middle, normed_two, upward, active))


def backward(incoming, cache, weights):
    gains, biases, w_qkv, w_out, w_up, w_down = weights
    hidden, normed, project, probs, context, middle, normed_two, upward, active = cache
    row_count = hidden.shape[0]
    scale = 1.0 / math.sqrt(HEAD_DIM)
    grad_down = jnp.einsum("rf,rd->fd", active, incoming, preferred_element_type=jnp.float32)
    grad_active = jnp.einsum("rd,fd->rf", incoming, w_down, preferred_element_type=jnp.float32)
    unused, gelu_pull = jax.vjp(gelu_tanh, upward)
    grad_upward = gelu_pull(grad_active)[0].astype(jnp.bfloat16)
    grad_up = jnp.einsum("rm,rf->mf", normed_two, grad_upward, preferred_element_type=jnp.float32)
    grad_normed_two = jnp.einsum("rf,mf->rm", grad_upward, w_up, preferred_element_type=jnp.float32)
    unused, second_pull = jax.vjp(normalize, middle, gains[1], biases[1])
    grad_middle_norm, grad_gain_two, grad_bias_two = second_pull(grad_normed_two)
    grad_middle = incoming.astype(jnp.float32) + grad_middle_norm
    grad_attended = grad_middle.astype(jnp.bfloat16)
    grad_wout = jnp.einsum("rm,rn->mn", context, grad_attended, preferred_element_type=jnp.float32)
    grad_context = jnp.einsum("rn,mn->rm", grad_attended, w_out, preferred_element_type=jnp.float32)
    grad_context = grad_context.astype(jnp.bfloat16).reshape(row_count, HEADS, HEAD_DIM)
    shaped = project.reshape(row_count, 3, HEADS, HEAD_DIM)
    grad_probs = jnp.einsum(
        "rhd,chd->hrc", grad_context, shaped[:, 2], preferred_element_type=jnp.float32
    )
    grad_values = jnp.einsum(
        "hrc,rhd->chd", probs.astype(jnp.bfloat16), grad_context, preferred_element_type=jnp.float32
    )
    grad_scores = probs * (grad_probs - jnp.sum(probs * grad_probs, axis=-1, keepdims=True))
    grad_scores = grad_scores.astype(jnp.bfloat16)
    grad_queries = (
        jnp.einsum("hrc,chd->rhd", grad_scores, shaped[:, 1], preferred_element_type=jnp.float32)
        * scale
    )
    grad_keys = (
        jnp.einsum("hrc,rhd->chd", grad_scores, shaped[:, 0], preferred_element_type=jnp.float32)
        * scale
    )
    grad_project = jnp.stack([grad_queries, grad_keys, grad_values], axis=1)
    grad_project = grad_project.reshape(row_count, 3 * HEADS * HEAD_DIM).astype(jnp.bfloat16)
    grad_wqkv = jnp.einsum("rm,rn->mn", normed, grad_project, preferred_element_type=jnp.float32)
    grad_normed = jnp.einsum("rn,mn->rm", grad_project, w_qkv, preferred_element_type=jnp.float32)
    unused, first_pull = jax.vjp(normalize, hidden, gains[0], biases[0])
    grad_hidden_norm, grad_gain_one, grad_bias_one = first_pull(grad_normed)
    grad_hidden = (grad_middle + grad_hidden_norm).astype(jnp.bfloat16)
    gain_grads = jnp.stack([grad_gain_one, grad_gain_two])
    bias_grads = jnp.stack([grad_bias_one, grad_bias_two])
    return (grad_hidden, (gain_grads, bias_grads, grad_wqkv, grad_wout, grad_up, grad_down))


def on_device(tokens, cotangent, norm_gains, norm_biases, w_qkv, w_out, w_up, w_down):
    weights = (norm_gains[0], norm_biases[0], w_qkv[0], w_out[0], w_up[0], w_down[0])
    section_index = lax.axis_index("section")
    is_first = section_index == 0
    width = tokens.shape[1]
    row_count = tokens.shape[0] // MICRO
    pieces = tokens.reshape(MICRO, row_count, width)
    cot_pieces = cotangent.reshape(MICRO, row_count, width)
    outgoing = jnp.zeros((row_count, width), jnp.bfloat16)
    saved = []
    produced = []
    for moment in range(MICRO + 1):
        arrived = passed_along(outgoing, "section", 1)
        own_piece = pieces[min(moment, MICRO - 1)]
        inputs = jnp.where(is_first, own_piece, arrived)
        outgoing, cache = forward(inputs, weights)
        saved.append(inputs)
        produced.append(outgoing)
    mixed = lax.dynamic_slice_in_dim(jnp.stack(produced), section_index, MICRO, 0)
    mixed = mixed.reshape(1, MICRO * row_count, width)
    totals = tuple((jnp.zeros(member.shape, jnp.float32) for member in weights))
    shares = None
    returning = jnp.zeros((row_count, width), jnp.bfloat16)
    returned = []
    for moment in range(MICRO + 1):
        arrived = passed_along(returning, "section", -1)
        if moment < MICRO:
            target = cot_pieces[MICRO - 1 - moment]
        else:
            target = jnp.zeros((row_count, width), jnp.bfloat16)
        incoming = jnp.where(is_first, arrived, target)
        index = MICRO - moment
        unused, cache = forward(saved[index], weights)
        returning, gradients = backward(incoming, cache, weights)
        returned.append(returning)
        totals = tuple((left + right for left, right in zip(totals, gradients)))
    shares = (
        lax.psum_scatter(totals[0], "dp", scatter_dimension=1, tiled=True),
        lax.psum_scatter(totals[1], "dp", scatter_dimension=1, tiled=True),
        lax.psum_scatter(totals[2], "dp", scatter_dimension=0, tiled=True),
        lax.psum_scatter(totals[3], "dp", scatter_dimension=1, tiled=True),
        lax.psum_scatter(totals[4], "dp", scatter_dimension=0, tiled=True),
        lax.psum_scatter(totals[5], "dp", scatter_dimension=1, tiled=True),
    )
    grad_inputs = lax.dynamic_slice_in_dim(jnp.stack(returned[::-1]), section_index, MICRO, 0)
    grad_inputs = grad_inputs.reshape(1, MICRO * row_count, width)
    gain_share, bias_share, qkv_share, out_share, up_share, down_share = shares
    return (
        mixed,
        grad_inputs,
        qkv_share[None],
        out_share[None],
        up_share[None],
        down_share[None],
        gain_share[None],
        bias_share[None],
    )


def solution(mesh):
    placed = (
        P("dp", None),
        P("dp", None),
        P("section", None, None),
        P("section", None, None),
        P("section", None, None),
        P("section", None, None),
        P("section", None, None),
        P("section", None, None),
    )
    return jax.shard_map(
        on_device,
        mesh=mesh,
        in_specs=placed,
        out_specs=(
            P("section", "dp", None),
            P("section", "dp", None),
            P("section", "dp", None),
            P("section", None, "dp"),
            P("section", "dp", None),
            P("section", None, "dp"),
            P("section", None, "dp"),
            P("section", None, "dp"),
        ),
        check_vma=False,
    )
```

profile of v0, /device:TPU:0, one launch (start us, length us, event | category | flops | bytes accessed | tf_op | source)
XLA Modules:
  0.0 814.5 jit_solution(17936304464206282635)
XLA Ops:
  7.9 4.8 collective-permute-start
  14.5 3.8 collective-permute-done
  19.7 3.9 fusion.112
  28.6 3.6 fusion.63
  33.9 4.3 collective-permute-start.1
  38.2 4.3 collective-permute-done.1
  47.8 3.5 fusion.61
  52.9 4.9 collective-permute-start.2
  57.8 3.2 collective-permute-done.2
  70.9 3.7 fusion.59
  76.3 4.4 collective-permute-start.3
  94.2 3.1 fusion.57
  99.0 4.6 collective-permute-start.4
  112.6 2.4 fusion.210
  117.0 3.0 fusion.55
  134.5 5.4 fusion.460
  142.4 2.7 fusion.352
  145.1 3.9 collective-permute-done.6
  164.4 5.4 fusion.459
  172.3 2.7 fusion.355
  175.0 3.8 collective-permute-done.7
  194.1 5.4 fusion.458
  202.2 2.7 fusion.358
  205.0 3.6 collective-permute-done.8
  223.8 5.4 fusion.457
  231.7 2.7 fusion.361
  234.4 3.9 collective-permute-done.9
  251.4 5.1 fusion.456
  259.3 8.9 %add_add_fusion.3 = f32[1024,1024]{0,1:T(8,128)} fusion(f32[1024,1024]{0,1:T(8,128)} %fusion.361, f32[1024,1024]{0,1:T(8,128)} %fusion.358, f32[1024,1024]{0,1:T(8,128)} %fusion.352, f32[1024,1024]{0,1:T(8,128)} %fusion.355, bf16[120,1024]{1,0:T(8,128)(2,1)S(1)} %copy-done.82, bf16[8,15,8,128]{3,2,1,0:T(8,128)(2,1)S(1)} %copy-done.122), kind=kOutput, calls=%fused_computation.68 | convolution fusion | flops 255852544 | bytes 21463040 | tf_op jit(solution)/shard_map/rm,rn->mn/dot_general | solution.py:85
  271.8 4.5 fusion.454
  276.4 4.5 fusion.453
  280.9 4.5 fusion.452
  285.4 12.9 %add_add_fusion.1 = f32[2048,1024]{0,1:T(8,128)} fusion(f32[2048,1024]{0,1:T(8,128)} %fusion.452, f32[2048,1024]{0,1:T(8,128)} %fusion.453, f32[2048,1024]{0,1:T(8,128)S(1)} %fusion.455, f32[2048,1024]{0,1:T(8,128)} %fusion.454, bf16[120,1024]{1,0:T(8,128)(2,1)} %copy-done.72, pred[]{:T(512)S(6)} %eq.23, f32[120,2048]{1,0:T(8,128)S(1)} %copy-done.71), kind=kOutput, calls=%fused_computation.6 | convolution fusion | flops 514039808 | bytes 43171840 | tf_op jit(solution)/shard_map/rf,rd->fd/dot_general | solution.py:75
  299.4 2.5 fusion.451
  301.9 4.6 fusion.450
  306.5 4.6 fusion.449
  311.2 4.6 fusion.448
  315.8 12.9 %add_add_fusion.2 = f32[1024,2048]{1,0:T(8,128)} fusion(f32[1024,2048]{1,0:T(8,128)} %fusion.448, f32[1024,2048]{1,0:T(8,128)} %fusion.449, f32[1024,2048]{1,0:T(8,128)S(1)} %fusion.451, f32[1024,2048]{1,0:T(8,128)} %fusion.450, bf16[120,2048]{1,0:T(8,128)(2,1)S(1)} %copy-done.84, f32[120,1024]{1,0:T(8,128)S(1)} %copy-done.27, f32[1024]{0:T(1024)S(1)} %bitcast.696, ...), kind=kOutput, calls=%fused_computation.7 | convolution fusion | flops 512319488 | bytes 42935232 | tf_op jit(solution)/shard_map/rm,rf->mf/dot_general | solution.py:79
  329.9 6.5 fusion.277
  336.5 6.4 fusion.274
  343.0 6.6 fusion.271
  349.5 6.4 fusion.268
  355.9 21.9 %add_add_fusion = f32[1024,3072]{1,0:T(8,128)} fusion(f32[1024,3072]{1,0:T(8,128)} %fusion.268, f32[1024,3072]{1,0:T(8,128)} %fusion.271, f32[1024,3072]{1,0:T(8,128)} %fusion.277, f32[1024,3072]{1,0:T(8,128)} %fusion.274, bf16[15,8,24,128]{3,2,1,0:T(8,128)(2,1)S(1)} %bitcast.643, bf16[120,1024]{1,0:T(8,128)(2,1)S(1)} %copy-done.23, f32[1024]{0:T(1024)S(1)} %bitcast.661, ...), kind=kOutput, calls=%fused_computation.5 | convolution fusion | flops 768294912 | bytes 63906752 | tf_op jit(solution)/shard_map/rm,rn->mn/dot_general | solution.py:107
  378.9 4.2 fusion.203
  390.8 58.6 %reduce-scatter.13.cloned.1.call-done = f32[1024,64]{0,1:T(8,128)} async-done(((f32[1024,1024]{0,1:T(8,128)}), f32[1024,64]{0,1:T(8,128)}) %reduce-scatter.13.cloned.1.call-update) | async-done | bytes 262160 | tf_op jit(solution)/shard_map/reduce_scatter | solution.py:157
  449.4 108.7 %reduce-scatter.17.cloned.1.call-done = f32[2048,64]{0,1:T(8,128)} async-done(((f32[2048,1024]{0,1:T(8,128)}), f32[2048,64]{0,1:T(8,128)}) %reduce-scatter.17.cloned.1.call-update) | async-done | bytes 524304 | tf_op jit(solution)/shard_map/reduce_scatter | solution.py:159
  558.2 109.5 %reduce-scatter.15.cloned.1.call-done = f32[64,2048]{1,0:T(8,128)} async-done(((f32[1024,2048]{1,0:T(8,128)}), f32[64,2048]{1,0:T(8,128)}) %reduce-scatter.15.cloned.1.call-update) | async-done | bytes 524304 | tf_op jit(solution)/shard_map/reduce_scatter | solution.py:158
  667.6 139.6 %reduce-scatter.11.cloned.1.call-done = f32[64,3072]{1,0:T(8,128)} async-done(((f32[1024,3072]{1,0:T(8,128)}), f32[64,3072]{1,0:T(8,128)}) %reduce-scatter.11.cloned.1.call-update) | async-done | bytes 786448 | tf_op jit(solution)/shard_map/reduce_scatter | solution.py:156
  (513 shorter events, 154.4 us)
Async XLA Ops:
  7.2 20.6 %copy-start = (bf16[1,1024,1024]{2,1,0:T(8,128)(2,1)S(1)}, bf16[1,1024,1024]{2,1,0:T(8,128)(2,1)}, u32[]{:S(2)}) copy-start(bf16[1,1024,1024]{2,1,0:T(8,128)(2,1)} %param.13) | copy-start | bytes 6291460
  7.2 380.8 %reduce-scatter.19.cloned.1.call-start = ((), (), s32[]{:S(2)}) async-start(), calls=%async_computation.10 | async-start | bytes 557056
  7.9 10.3 %collective-permute-start = (bf16[120,1024]{1,0:T(8,128)(2,1)}, bf16[120,1024]{1,0:T(8,128)(2,1)S(1)}, u32[]{:S(2)}, u32[]{:S(2)}) collective-permute-start(bf16[120,1024]{1,0:T(8,128)(2,1)} %broadcast.404), channel_id=1, source_target_pairs={{0,16},{1,17},{2,18},{3,19},{4,20},{5,21},{6,22},{7,23},{8,24},{9,... | collective-permute-start | bytes 737288 | tf_op jit(solution)/shard_map/ppermute | solution.py:20
  19.4 8.3 %copy-start.22 = (bf16[120,1024]{1,0:T(8,128)(2,1)}, bf16[120,1024]{1,0:T(8,128)(2,1)S(1)}, u32[]{:S(2)}) copy-start(bf16[120,1024]{1,0:T(8,128)(2,1)S(1)} %get-tuple-element.62) | copy-start | bytes 737284
  27.8 16.1 %slice-start = ((s8[6291456]{0:T(1024)(128)(4,1)}), s8[4194304]{0:T(1024)(128)(4,1)S(1)}, s32[]{:S(2)}) async-start(s8[6291456]{0:T(1024)(128)(4,1)} %bitcast.609), calls=%async_computation.12 | async-start | bytes 8388608
  28.6 15.3 %slice-start.1 = ((s8[6291456]{0:T(1024)(128)(4,1)}), s8[2097152]{0:T(1024)(128)(4,1)S(1)}, s32[]{:S(2)}) async-start(s8[6291456]{0:T(1024)(128)(4,1)} %bitcast.609), calls=%async_computation.13 | async-start | bytes 4194304
  33.9 8.6 %collective-permute-start.1 = (bf16[120,1024]{1,0:T(8,128)(2,1)S(1)}, bf16[120,1024]{1,0:T(8,128)(2,1)S(1)}, u32[]{:S(2)}, u32[]{:S(2)}) collective-permute-start(bf16[120,1024]{1,0:T(8,128)(2,1)S(1)} %get-tuple-element.87), channel_id=1, source_target_pairs={{0,16},{1,17},{2,18},{3,19},{4,20},{5,21},{6,22},{7,23},{8,24},{9,... | collective-permute-start | bytes 737288 | tf_op jit(solution)/shard_map/ppermute | solution.py:20
  47.0 15.4 %slice-start.2 = ((s8[6291456]{0:T(1024)(128)(4,1)}), s8[4194304]{0:T(1024)(128)(4,1)S(1)}, s32[]{:S(2)}) async-start(s8[6291456]{0:T(1024)(128)(4,1)} %bitcast.611), calls=%async_computation.14 | async-start | bytes 8388608
  47.8 14.6 %slice-start.3 = ((s8[6291456]{0:T(1024)(128)(4,1)}), s8[2097152]{0:T(1024)(128)(4,1)S(1)}, s32[]{:S(2)}) async-start(s8[6291456]{0:T(1024)(128)(4,1)} %bitcast.611), calls=%async_computation.15 | async-start | bytes 4194304
  52.9 8.1 collective-permute-start.2
  68.9 16.8 %slice-start.4 = ((s8[6291456]{0:T(1024)(128)(4,1)}), s8[4194304]{0:T(1024)(128)(4,1)S(1)}, s32[]{:S(2)}) async-start(s8[6291456]{0:T(1024)(128)(4,1)} %bitcast.613), calls=%async_computation.16 | async-start | bytes 8388608
  70.9 14.8 %slice-start.5 = ((s8[6291456]{0:T(1024)(128)(4,1)}), s8[2097152]{0:T(1024)(128)(4,1)S(1)}, s32[]{:S(2)}) async-start(s8[6291456]{0:T(1024)(128)(4,1)} %bitcast.613), calls=%async_computation.17 | async-start | bytes 4194304
  76.3 8.1 collective-permute-start.3
  80.7 22.9 %collective-permute-start.5 = (bf16[120,1024]{1,0:T(8,128)(2,1)}, bf16[120,1024]{1,0:T(8,128)(2,1)}, u32[]{:S(2)}, u32[]{:S(2)}) collective-permute-start(bf16[120,1024]{1,0:T(8,128)(2,1)} %broadcast.404), channel_id=1, source_target_pairs={{16,0},{17,1},{18,2},{19,3},{20,4},{21,5},{22,6},{23,7},{24,8},{25... | collective-permute-start | bytes 737288 | tf_op jit(solution)/shard_map/ppermute | solution.py:20
  94.2 14.3 %slice-start.6 = ((s8[6291456]{0:T(1024)(128)(4,1)}), s8[4194304]{0:T(1024)(128)(4,1)S(1)}, s32[]{:S(2)}) async-start(s8[6291456]{0:T(1024)(128)(4,1)} %bitcast.615), calls=%async_computation.18 | async-start | bytes 8388608
  97.4 8.0 copy-start.44
  97.4 11.1 %slice-start.7 = ((s8[6291456]{0:T(1024)(128)(4,1)}), s8[2097152]{0:T(1024)(128)(4,1)S(1)}, s32[]{:S(2)}) async-start(s8[6291456]{0:T(1024)(128)(4,1)} %bitcast.615), calls=%async_computation.19 | async-start | bytes 4194304
  99.0 8.1 collective-permute-start.4
  139.9 10.0 %copy-start.45 = (f32[120,2048]{1,0:T(8,128)S(1)}, f32[120,2048]{1,0:T(8,128)}, u32[]{:S(2)}) copy-start(f32[120,2048]{1,0:T(8,128)} %copy-done.44) | copy-start | bytes 2949124
  139.9 10.0 %copy-start.139 = (bf16[1,2048,1024]{2,1,0:T(8,128)(2,1)S(1)}, bf16[1,2048,1024]{2,1,0:T(8,128)(2,1)}, u32[]{:S(2)}) copy-start(bf16[1,2048,1024]{2,1,0:T(8,128)(2,1)} %param.15) | copy-start | bytes 12582916
  140.6 8.4 %collective-permute-start.6 = (bf16[120,1024]{1,0:T(8,128)(2,1)S(1)}, bf16[120,1024]{1,0:T(8,128)(2,1)S(1)}, u32[]{:S(2)}, u32[]{:S(2)}) collective-permute-start(bf16[120,1024]{1,0:T(8,128)(2,1)S(1)} %add_convert_fusion.4), channel_id=1, source_target_pairs={{16,0},{17,1},{18,2},{19,3},{20,4},{21,5},{22,6},{23,7},{24,8},{25... | collective-permute-start | bytes 737288 | tf_op jit(solution)/shard_map/ppermute | solution.py:20
  164.4 7.9 copy-start.76
  164.4 7.9 copy-start.113
  169.8 10.0 %copy-start.42 = (f32[120,2048]{1,0:T(8,128)S(1)}, f32[120,2048]{1,0:T(8,128)}, u32[]{:S(2)}) copy-start(f32[120,2048]{1,0:T(8,128)} %copy-done.41) | copy-start | bytes 2949124
  169.8 10.0 %copy-start.140 = (bf16[1,2048,1024]{2,1,0:T(8,128)(2,1)S(1)}, bf16[1,2048,1024]{2,1,0:T(8,128)(2,1)}, u32[]{:S(2)}) copy-start(bf16[1,2048,1024]{2,1,0:T(8,128)(2,1)} %param.15) | copy-start | bytes 12582916
  170.5 11.5 %copy-start.94 = (bf16[120,1024]{1,0:T(8,128)(2,1)}, bf16[120,1024]{1,0:T(8,128)(2,1)S(1)}, u32[]{:S(2)}) copy-start(bf16[120,1024]{1,0:T(8,128)(2,1)S(1)} %add_convert_fusion.3) | copy-start | bytes 737284
  170.5 8.4 %collective-permute-start.7 = (bf16[120,1024]{1,0:T(8,128)(2,1)S(1)}, bf16[120,1024]{1,0:T(8,128)(2,1)S(1)}, u32[]{:S(2)}, u32[]{:S(2)}) collective-permute-start(bf16[120,1024]{1,0:T(8,128)(2,1)S(1)} %add_convert_fusion.3), channel_id=1, source_target_pairs={{16,0},{17,1},{18,2},{19,3},{20,4},{21,5},{22,6},{23,7},{24,8},{25... | collective-permute-start | bytes 737288 | tf_op jit(solution)/shard_map/ppermute | solution.py:20
  194.1 8.1 copy-start.78
  194.1 8.1 copy-start.109
  199.5 10.0 %copy-start.37 = (f32[120,2048]{1,0:T(8,128)S(1)}, f32[120,2048]{1,0:T(8,128)}, u32[]{:S(2)}) copy-start(f32[120,2048]{1,0:T(8,128)} %copy-done.36) | copy-start | bytes 2949124
  199.5 10.0 %copy-start.141 = (bf16[1,2048,1024]{2,1,0:T(8,128)(2,1)S(1)}, bf16[1,2048,1024]{2,1,0:T(8,128)(2,1)}, u32[]{:S(2)}) copy-start(bf16[1,2048,1024]{2,1,0:T(8,128)(2,1)} %param.15) | copy-start | bytes 12582916
  200.2 11.5 %copy-start.96 = (bf16[120,1024]{1,0:T(8,128)(2,1)}, bf16[120,1024]{1,0:T(8,128)(2,1)S(1)}, u32[]{:S(2)}) copy-start(bf16[120,1024]{1,0:T(8,128)(2,1)S(1)} %add_convert_fusion.2) | copy-start | bytes 737284
  200.2 8.4 %collective-permute-start.8 = (bf16[120,1024]{1,0:T(8,128)(2,1)S(1)}, bf16[120,1024]{1,0:T(8,128)(2,1)S(1)}, u32[]{:S(2)}, u32[]{:S(2)}) collective-permute-start(bf16[120,1024]{1,0:T(8,128)(2,1)S(1)} %add_convert_fusion.2), channel_id=1, source_target_pairs={{16,0},{17,1},{18,2},{19,3},{20,4},{21,5},{22,6},{23,7},{24,8},{25... | collective-permute-start | bytes 737288 | tf_op jit(solution)/shard_map/ppermute | solution.py:20
  229.2 9.1 %copy-start.70 = (f32[120,2048]{1,0:T(8,128)S(1)}, f32[120,2048]{1,0:T(8,128)}, u32[]{:S(2)}) copy-start(f32[120,2048]{1,0:T(8,128)} %copy-done.69) | copy-start | bytes 2949124
  229.2 9.1 %copy-start.142 = (bf16[1,2048,1024]{2,1,0:T(8,128)(2,1)S(1)}, bf16[1,2048,1024]{2,1,0:T(8,128)(2,1)}, u32[]{:S(2)}) copy-start(bf16[1,2048,1024]{2,1,0:T(8,128)(2,1)} %param.15) | copy-start | bytes 12582916
  229.9 8.4 %collective-permute-start.9 = (bf16[120,1024]{1,0:T(8,128)(2,1)S(1)}, bf16[120,1024]{1,0:T(8,128)(2,1)S(1)}, u32[]{:S(2)}, u32[]{:S(2)}) collective-permute-start(bf16[120,1024]{1,0:T(8,128)(2,1)S(1)} %add_convert_fusion.1), channel_id=1, source_target_pairs={{16,0},{17,1},{18,2},{19,3},{20,4},{21,5},{22,6},{23,7},{24,8},{25... | collective-permute-start | bytes 737288 | tf_op jit(solution)/shard_map/ppermute | solution.py:20
  251.4 7.9 copy-start.82
  251.4 7.9 copy-start.122
  258.1 131.4 %reduce-scatter.21.cloned.1.call-start = ((), (), s32[]{:S(2)}) async-start(), calls=%async_computation.11 | async-start | bytes 557056
  259.2 190.2 %reduce-scatter.13.cloned.1.call-start = ((), (), s32[]{:S(2)}) async-start(), calls=%async_computation.7 | async-start | bytes 4456448 | tf_op jit(solution)/shard_map/reduce_scatter | solution.py:157
  268.2 289.9 %reduce-scatter.17.cloned.1.call-start = ((), (), s32[]{:S(2)}) async-start(), calls=%async_computation.9 | async-start | bytes 8912896 | tf_op jit(solution)/shard_map/reduce_scatter | solution.py:159
  298.4 369.3 %reduce-scatter.15.cloned.1.call-start = ((), (), s32[]{:S(2)}) async-start(), calls=%async_computation.8 | async-start | bytes 8912896 | tf_op jit(solution)/shard_map/reduce_scatter | solution.py:158
  328.7 478.5 %reduce-scatter.11.cloned.1.call-start = ((), (), s32[]{:S(2)}) async-start(), calls=%async_computation.6 | async-start | bytes 13369344 | tf_op jit(solution)/shard_map/reduce_scatter | solution.py:156
  378.9 8.0 copy-start.99
  378.9 8.0 copy-start.97
  378.9 8.1 copy-start.95
  378.9 8.1 copy-start.93
  378.9 428.3 %copy-start.1 = (bf16[1,1024,1024]{2,1,0:T(8,128)(2,1)S(1)}, bf16[1,1024,1024]{2,1,0:T(8,128)(2,1)}, u32[]{:S(2)}) copy-start(bf16[1,1024,1024]{2,1,0:T(8,128)(2,1)} %param.13) | copy-start | bytes 6291460
  (119 other events, 463.2 us)
Sparse Core Ops, SparseCore 0:
  258.2 56.0 reduce-scatter.18
  318.3 54.7 reduce-scatter.20
  377.6 71.7 reduce-scatter.12
  454.5 103.6 reduce-scatter.16
  563.2 104.4 reduce-scatter.14
  672.7 134.5 reduce-scatter.10
where the time goes:
time: 823 us; the launch traced here: 815 us
  waiting for transfers between devices  447 us (54%)
  matrix products  258 us (31%)
  starting transfers between devices  32.3 us (4%)
  local copies, waits for them, and re-layouts  30.9 us (4%)
  other arithmetic  29.7 us (4%)
  between operations  17 us (2%)
    reduce_scatter x1, waiting for transfers between devices, on_device(): lax.psum_scatter(totals[2], 'dp', scatter_dimension=0, tiled=True)  140 us
    reduce_scatter x1, waiting for transfers between devices, on_device(): lax.psum_scatter(totals[4], 'dp', scatter_dimension=0, tiled=True)  109 us
    reduce_scatter x1, waiting for transfers between devices, on_device(): lax.psum_scatter(totals[5], 'dp', scatter_dimension=1, tiled=True)  109 us
    reduce_scatter x1, waiting for transfers between devices, on_device(): lax.psum_scatter(totals[3], 'dp', scatter_dimension=1, tiled=True)  58.6 us
    dot_general x5, matrix products, backward(): jnp.einsum('rm,rn->mn', normed, grad_project, preferred_element_type=jnp....  47.9 us
    ppermute x10, starting transfers between devices, passed_along(): return lax.ppermute(block, axis, route)  31.6 us
    ppermute x10, waiting for transfers between devices, passed_along(): return lax.ppermute(block, axis, route)  30.5 us
    dot_general x5, matrix products, backward(): jnp.einsum('rm,rf->mf', normed_two, grad_upward, preferred_element_type=j...  29.3 us
  transfers between devices with their start and end apart: 16, of which 13 were waited for; matrix products, arithmetic and copies ran while one was open for 19% of the time, Pallas kernels for 0%

commit v1 on v0

v1 whole, which is shorter than its diff:
```python
import math

import jax
import jax.numpy as jnp
from jax import lax
from jax.experimental import pallas as pl
from jax.experimental.pallas import tpu as pltpu
from jax.sharding import PartitionSpec as P

HEADS = 8
HEAD_DIM = 128
ITEM_LEN = 15
MICRO = 2
EPSILON = 1e-05

LINE, PAIR, CORES = 4, 2, 2
GROUP = LINE * PAIR * CORES
PANEL = 256
AHEAD = 4
RING = 4
MESH = pl.DeviceIdType.MESH
BF16, F32 = jnp.bfloat16, jnp.float32
DOWN, UP, OUT, QKV = range(4)


def dot(left, right):
    return jnp.dot(left, right, preferred_element_type=F32)


def dot_nt(left, right):
    return lax.dot_general(left, right, (((1,), (1,)), ((), ())), preferred_element_type=F32)


def dot_tn(left, right):
    return lax.dot_general(left, right, (((0,), (0,)), ((), ())), preferred_element_type=F32)


def normalized(values):
    centered = values - jnp.mean(values, axis=-1, keepdims=True)
    scale = lax.rsqrt(jnp.mean(centered * centered, axis=-1, keepdims=True) + EPSILON)
    return centered * scale, scale


def normalize_back(grad, unit, scale, gain):
    scaled = grad * gain
    along = jnp.mean(scaled * unit, axis=-1, keepdims=True)
    return scale * (scaled - jnp.mean(scaled, axis=-1, keepdims=True) - unit * along)


def gelu_parts(u):
    square = u * u
    inner = jnp.tanh(0.7978845608 * u * (1.0 + 0.044715 * square))
    return square, inner


def gelu(u):
    unused, inner = gelu_parts(u)
    return 0.5 * u * (1.0 + inner)


def gelu_slope(u):
    square, inner = gelu_parts(u)
    steep = 0.7978845608 * (1.0 + 3 * 0.044715 * square)
    return 0.5 * (1.0 + inner) + 0.5 * u * (1.0 - inner * inner) * steep


def layer_kernel(
    tokens_in, cotangent_in, gains, biases, w_qkv_in, w_out_in, w_up_in, w_down_in,
    mixed_out, grads_out, out, vector_out, buf, sem,
):
    h, e, result = buf["h"], buf["e"], buf["result"]
    w_qkv, w_out, w_up, w_down = buf["w_qkv"], buf["w_out"], buf["w_up"], buf["w_down"]
    left, e_half, right, twin_right = buf["left"], buf["e_half"], buf["right"], buf["twin_right"]
    act_beside, proj, middle, up = buf["act_beside"], buf["proj"], buf["middle"], buf["up"]
    probs, bias, dctx, vector = buf["probs"], buf["bias"], buf["dctx"], buf["vector"]
    parts, acc, fin = buf["parts"], buf["acc"], buf["fin"]
    pair_beside, pair_in, pair_across = buf["pair_beside"], buf["pair_in"], buf["pair_across"]
    vectors = buf["vectors"]

    all_rows, width = h.shape
    rows = all_rows // MICRO
    hidden = w_up.shape[1]
    chunk, half_chunk = acc.shape[2], acc.shape[2] // 2
    widths = (hidden, hidden, width, 3 * width)
    columns_at = (0, hidden, 2 * hidden, 2 * hidden + width)
    starts = [0]
    for member in widths:
        starts.append(starts[-1] + member // CORES // PANEL)
    panels, direct = starts[-1], starts[1]
    halves = [member // CORES for member in widths]
    twin_at = [start * PANEL for start in starts]

    section = lax.axis_index("section")
    place = lax.axis_index("dp")
    first = (place // GROUP) * GROUP
    mine = place - first
    z, y, core = mine // (PAIR * CORES), (mine // CORES) % PAIR, mine % CORES
    other_y, other_core = 1 - y, 1 - core
    far_side = z // 2
    is_end = (z == 0) | (z == LINE - 1)
    is_inner = jnp.logical_not(is_end)
    own = jnp.where(is_end, 0, 1)

    def numbered(zz):
        return zz + far_side * (LINE - 1 - 2 * zz)

    def device(zz, yy, cc):
        return (section, first + (zz * PAIR + yy) * CORES + cc)

    inner, end, across = (device(numbered(zz), y, core) for zz in (1, 0, 2))
    beside, twin = device(z, other_y, core), device(z, y, other_core)
    partner = (1 - section, place)
    leads = section == 0

    def send(source, target, key, index, to):
        return pltpu.make_async_remote_copy(
            src_ref=source, dst_ref=target, send_sem=sem[key + "_send"].at[index],
            recv_sem=sem[key + "_recv"].at[index], device_id=to, device_id_type=MESH,
        )

    def fetch(source, target, index):
        return pltpu.make_async_copy(source, target, sem["fetch"].at[index])

    def rows_of(m):
        return pl.ds(pl.multiple_of(m * rows, rows), rows)

    loads = [
        fetch(w_qkv_in, w_qkv, 0), fetch(w_out_in, w_out, 1), fetch(w_up_in, w_up, 2), fetch(w_down_in, w_down, 3),
    ]

    @pl.when(leads)
    def _():
        fetch(tokens_in, h, 4).start()

    @pl.when(jnp.logical_not(leads))
    def _():
        fetch(cotangent_in, e, 4).start()

    loads[0].start()
    barrier = pltpu.get_barrier_semaphore()
    pl.semaphore_signal(barrier, inc=1, device_id=partner, device_id_type=MESH)
    for step in range(1, GROUP):
        peer = (section, first + (mine + step) % GROUP)
        pl.semaphore_signal(barrier, inc=1, device_id=peer, device_id_type=MESH)

    row_ids = lax.broadcasted_iota(jnp.int32, (rows, rows), 0)
    col_ids = lax.broadcasted_iota(jnp.int32, (rows, rows), 1)
    seen = (row_ids // ITEM_LEN == col_ids // ITEM_LEN) & (col_ids <= row_ids)
    bias[...] = jnp.where(seen, 0.0, -1e30)
    vector[...] = jnp.zeros_like(vector)
    scale = 1.0 / math.sqrt(HEAD_DIM)

    pl.semaphore_wait(barrier, GROUP)
    fetch(tokens_in, h, 4).wait()


    def x_forward(m):
        return send(result.at[rows_of(m)], h.at[rows_of(m)], "x_forward", m, partner)

    def x_back(m):
        return send(h.at[rows_of(m)], e.at[rows_of(m)], "x_back", m, partner)

    def mixed_store(m):
        return pltpu.make_async_copy(result.at[rows_of(m)], mixed_out.at[rows_of(m)], sem["store"].at[0, m])

    def grads_store(m):
        return pltpu.make_async_copy(h.at[rows_of(m)], grads_out.at[rows_of(m)], sem["store"].at[1, m])

    def twin_left(which, m):
        return send(left.at[which - 1, 0, rows_of(m)], left.at[which - 1, 1, rows_of(m)],
                    "twin_left", (which - 1, m), twin)

    def twin_right_of(which, m):
        start = pl.multiple_of(columns_at[which] + other_core * halves[which], 128)
        return send(right.at[rows_of(m), pl.ds(start, halves[which])],
                    twin_right.at[rows_of(m), pl.ds(twin_at[which], halves[which])],
                    "twin_right", (which, m), twin)

    def act_beside_of(source, m):
        if source == 0:
            start = pl.multiple_of(core * halves[DOWN], 128)
            held = right.at[rows_of(m), pl.ds(start, halves[DOWN])]
        else:
            held = twin_right.at[rows_of(m), pl.ds(0, halves[DOWN])]
        return send(held, act_beside.at[source, rows_of(m)], "act_beside", (source, m), beside)

    def e_twin(m):
        return send(e_half.at[0, rows_of(m)], e_half.at[1, rows_of(m)], "e_half", (0, m), twin)

    def e_beside(m):
        return send(result.at[rows_of(m), pl.ds(0, width // 2)], e_half.at[2, rows_of(m)], "e_half", (1, m), beside)

    def e_onward(m):
        return send(e_half.at[2, rows_of(m)], e_half.at[3, rows_of(m)], "e_half", (2, m), twin)


    def once(m, load, following=()):
        @pl.when(m == 0)
        def _():
            loads[load].wait()
            for other in following:
                loads[other].start()

    def forward(m):
        at = rows_of(m)
        unit, unused = normalized(h[at].astype(F32))
        left[QKV - 1, 0, at] = (unit * gains[0:1] + biases[0:1]).astype(BF16)
        once(m, 0, (1, 2, 3))
        for part in range(3):
            cols = slice(part * width, (part + 1) * width)
            proj[at, cols] = dot(left[QKV - 1, 0, at], w_qkv[:, cols]).astype(BF16)
        twin_left(QKV, m).start()

        @pl.loop(0, HEADS // 2)
        def _(pair):
            for member in range(2):
                head = pair * 2 + member
                q, k, v = (
                    proj[at, pl.ds(pl.multiple_of(part * width + head * HEAD_DIM, HEAD_DIM), HEAD_DIM)]
                    for part in range(3)
                )
                scores = dot_nt(q, k) * scale + bias[...]
                weight = jnp.exp(scores - jnp.max(scores, axis=-1, keepdims=True))
                weight = weight / jnp.sum(weight, axis=-1, keepdims=True)
                weight = weight.astype(BF16)
                probs[m * HEADS + head] = weight
                cols = pl.ds(pl.multiple_of(columns_at[OUT] + head * HEAD_DIM, HEAD_DIM), HEAD_DIM)
                right[at, cols] = dot(weight, v).astype(BF16)

        once(m, 1)
        twin_right_of(OUT, m).start()
        attended = dot(right[at, columns_at[OUT] : columns_at[OUT] + width], w_out[...])
        middle[at] = h[at].astype(F32) + attended
        unit, unused = normalized(middle[at])
        left[UP - 1, 0, at] = (unit * gains[1:2] + biases[1:2]).astype(BF16)
        twin_left(UP, m).start()
        once(m, 2)
        for part in range(2):
            cols = slice(part * hidden // 2, (part + 1) * hidden // 2)
            upward = dot(left[UP - 1, 0, at], w_up[:, cols])
            up[at, cols] = upward.astype(BF16)
            right[at, cols] = gelu(upward).astype(BF16)
        twin_right_of(DOWN, m).start()
        act_beside_of(0, m).start()
        once(m, 3)
        result[at] = (middle[at] + dot(right[at, :hidden], w_down[...])).astype(BF16)
        mixed_store(m).start()

        @pl.when(leads)
        def _():
            x_forward(m).start()

        twin_right_of(DOWN, m).wait_recv()
        act_beside_of(1, m).start()

    def backward(m, hook):
        at = rows_of(m)
        mixed_store(m).wait()

        @pl.when(leads)
        def _():
            x_forward(m).wait_send()

        for zz in range(LINE):
            cols = pl.ds(zz * chunk, chunk)
            e_half[0, at, cols] = e[at, pl.ds(pl.multiple_of((zz * PAIR + y) * chunk, chunk), chunk)]
            result[at, cols] = e[at, pl.ds(pl.multiple_of((zz * PAIR + other_y) * chunk, chunk), chunk)]
        e_beside(m).start()
        e_twin(m).start()
        for part in range(2):
            cols = slice(part * hidden // 2, (part + 1) * hidden // 2)
            passed = dot_nt(e[at], w_down[cols])
            slope = gelu_slope(up[at, cols].astype(F32))
            here = slice(columns_at[UP] + cols.start, columns_at[UP] + cols.stop)
            right[at, here] = (passed * slope).astype(BF16)
        twin_right_of(UP, m).start()
        grad = dot_nt(right[at, columns_at[UP] : columns_at[UP] + hidden], w_up[...])
        unit, size = normalized(middle[at])
        vector[1:2] += jnp.sum(grad * unit, axis=0, keepdims=True)
        vector[3:4] += jnp.sum(grad, axis=0, keepdims=True)
        middle[at] = e[at].astype(F32) + normalize_back(grad, unit, size, gains[1:2])
        left[OUT - 1, 0, at] = middle[at].astype(BF16)
        twin_left(OUT, m).start()
        dctx[...] = dot_nt(left[OUT - 1, 0, at], w_out[...]).astype(BF16)
        hook(m)

        @pl.loop(0, HEADS // 2)
        def _(pair):
            for member in range(2):
                head = pair * 2 + member
                q, k, v = (
                    proj[at, pl.ds(pl.multiple_of(part * width + head * HEAD_DIM, HEAD_DIM), HEAD_DIM)]
                    for part in range(3)
                )
                grad_ctx = dctx[:, pl.ds(pl.multiple_of(head * HEAD_DIM, HEAD_DIM), HEAD_DIM)]
                weight = probs[m * HEADS + head]
                grad_weight = dot_nt(grad_ctx, v)
                grad_v = dot_tn(weight, grad_ctx)
                weight = weight.astype(F32)
                total = jnp.sum(weight * grad_weight, axis=-1, keepdims=True)
                grad_scores = (weight * (grad_weight - total)).astype(BF16)
                grad_q = dot(grad_scores, k) * scale
                grad_k = dot_tn(grad_scores, q) * scale
                for part, value in enumerate((grad_q, grad_k, grad_v)):
                    start = columns_at[QKV] + part * width + head * HEAD_DIM
                    right[at, pl.ds(pl.multiple_of(start, HEAD_DIM), HEAD_DIM)] = value.astype(BF16)

        twin_right_of(QKV, m).start()
        grad = dot_nt(right[at, columns_at[QKV] : columns_at[QKV] + 3 * width], w_qkv[...])
        unit, size = normalized(h[at].astype(F32))
        vector[0:1] += jnp.sum(grad * unit, axis=0, keepdims=True)
        vector[2:3] += jnp.sum(grad, axis=0, keepdims=True)
        h[at] = (middle[at] + normalize_back(grad, unit, size, gains[0:1])).astype(BF16)
        grads_store(m).start()

        @pl.when(jnp.logical_not(leads))
        def _():
            x_back(m).start()


    def beside_of(p):
        i = p - direct
        return send(parts.at[i % AHEAD, :, other_y], pair_beside.at[i % (2 * AHEAD)], "pair_beside", i, beside)

    def in_of(p):
        return send(acc.at[p % RING, pl.ds(1, 3)], pair_in.at[p % RING], "pair_in", p, inner)

    def across_of(p):
        return send(acc.at[p % RING, pl.ds(2, 2)], pair_across.at[p % RING], "pair_across", p, across)

    def out_of(p):
        return send(acc.at[p % RING, 0], pair_in.at[p % RING, 0], "pair_out", p, end)

    def fin_of(p):
        return send(fin.at[p % RING], out.at[core, :, pl.ds(pl.multiple_of(p * PANEL, PANEL), PANEL)], "fin", p, twin)

    def add(target, *refs):
        total = target[...].astype(F32)
        for ref in refs:
            total = total + ref[...].astype(F32)
        target[...] = total.astype(BF16)

    def own_columns(p):
        place_of = p * PANEL + core * halves[0]
        for i in (1, 2, 3):
            shift = (columns_at[i] - twin_at[i] + core * halves[i]) - (
                columns_at[i - 1] - twin_at[i - 1] + core * halves[i - 1])
            place_of = place_of + jnp.where(p >= starts[i], shift, 0)
        return pl.ds(pl.multiple_of(place_of, 128), PANEL)

    def twin_columns(p):
        return pl.ds(pl.multiple_of(p * PANEL, PANEL), PANEL)

    def wait_for(which):
        for m in range(MICRO):
            twin_left(which, m).wait_recv()
            twin_right_of(which, m).wait_recv()

    def start_panel(p):
        which = 0
        for i in (OUT, QKV):
            which = which + (p >= starts[i]).astype(jnp.int32)

            @pl.when(p == starts[i])
            def _(i=i):
                wait_for(i)

        total = dot_tn(left[which, 0], right[:, own_columns(p)]) + dot_tn(left[which, 1], twin_right[:, twin_columns(p)])
        total = total.astype(BF16).reshape(parts.shape[1:])
        for zz in range(LINE):
            parts[(p - direct) % AHEAD, numbered(zz)] = total[zz]
        beside_of(p).start()

    def early():
        wait_for(UP)

        @pl.loop(direct, direct + AHEAD)
        def _(p):
            start_panel(p)

        for m in range(MICRO):
            e_beside(m).wait_recv()
            e_onward(m).start()
        for m in range(MICRO):
            e_twin(m).wait_recv()
            act_beside_of(0, m).wait_recv()
            act_beside_of(1, m).wait_recv()
            e_onward(m).wait_recv()

        @pl.loop(0, direct)
        def _(p):
            total = dot_tn(e_half[0], right[:, own_columns(p)]) + dot_tn(e_half[1], twin_right[:, twin_columns(p)])
            for source in range(2):
                total = total + dot_tn(e_half[2 + source], act_beside[source, :, twin_columns(p)])
            total = total.astype(BF16).reshape(acc.shape[1:])
            for zz in range(LINE):
                acc[p % RING, numbered(zz)] = total[zz]

            @pl.when(is_end & (p < 2))
            def _():
                in_of(p).start()

    def proceed(t):
        @pl.when((t < direct - 2) & is_end)
        def _():
            in_of(t + 2).start()

        @pl.when((t >= direct) & (t < panels))
        def _():
            i = t - direct
            beside_of(t).wait()
            for d in range(LINE):
                total = parts[i % AHEAD, d, y].astype(F32) + pair_beside[i % (2 * AHEAD), d].astype(F32)
                acc[t % RING, d] = total.astype(BF16)

            @pl.when(is_end)
            def _():
                in_of(t).start()

            @pl.when(t + AHEAD < panels)
            def _():
                start_panel(t + AHEAD)

        p = t - 1

        @pl.when((p >= 0) & (p < panels) & is_inner)
        def _():
            in_of(p).wait_recv()
            add(acc.at[p % RING, pl.ds(2, 2)], pair_in.at[p % RING, pl.ds(1, 2)])
            across_of(p).start()
            add(acc.at[p % RING, 1], pair_in.at[p % RING, 0])

        q = t - 2

        @pl.when((q >= 0) & (q < panels) & is_inner)
        def _():
            across_of(q).wait_recv()
            add(acc.at[q % RING, 0], pair_across.at[q % RING, 1])
            out_of(q).start()
            add(acc.at[q % RING, 1], pair_across.at[q % RING, 0])

        r = t - 3

        @pl.when(r >= 0)
        def _():
            @pl.when(is_end)
            def _():
                out_of(r).wait_recv()
                add(acc.at[r % RING, 0], pair_in.at[r % RING, 0])
                in_of(r).wait_send()

            @pl.when(is_inner)
            def _():
                across_of(r).wait_send()
                out_of(r).wait_send()

            def block(which):
                return acc[r % RING, own, pl.ds(pl.multiple_of(which * half_chunk, half_chunk), half_chunk)].astype(F32)

            @pl.when(r >= RING)
            def _():
                fin_of(r - RING).wait_send()

            fin[r % RING] = block(other_core)
            fin_of(r).start()
            out[core, :, twin_columns(r)] = block(core)


    def hook(m):
        @pl.when((m == MICRO - 1) & leads)
        def _():
            early()

    @pl.loop(0, 2 * MICRO)
    def _(step):
        m = step % MICRO

        @pl.when(step < MICRO)
        def _():
            @pl.when(jnp.logical_not(leads))
            def _():
                x_forward(m).wait_recv()

            forward(m)

        @pl.when(leads == (step >= MICRO))
        def _():
            @pl.when(leads)
            def _():
                x_back(m).wait_recv()

            backward(m, hook)

    def send_vector(step):
        peer = (mine + step) % GROUP
        start = pl.multiple_of((peer // CORES) * chunk, chunk)
        return pltpu.make_async_remote_copy(
            src_ref=vector.at[:, pl.ds(start, chunk)], dst_ref=vectors.at[mine],
            send_sem=sem["vector_send"].at[step], recv_sem=sem["vector_recv"].at[mine],
            device_id=(section, first + peer), device_id_type=MESH,
        )

    @pl.loop(1, GROUP)
    def _(step):
        send_vector(step).start()

    @pl.when(jnp.logical_not(leads))
    def _():
        early()

    @pl.loop(0, panels + 3)
    def _(t):
        proceed(t)

    vector_total = vector[:, pl.ds(pl.multiple_of((mine // CORES) * chunk, chunk), chunk)]
    for step in range(1, GROUP):
        sender = (mine + step) % GROUP
        pltpu.make_async_remote_copy(
            src_ref=vector.at[:, pl.ds(0, chunk)], dst_ref=vectors.at[sender],
            send_sem=sem["vector_send"].at[step], recv_sem=sem["vector_recv"].at[sender],
            device_id=twin, device_id_type=MESH,
        ).wait_recv()
        vector_total = vector_total + vectors[sender]
    vector_out[...] = vector_total

    @pl.loop(1, GROUP)
    def _(step):
        send_vector(step).wait_send()

    for m in range(MICRO):
        for which in (UP, OUT, QKV):
            twin_left(which, m).wait_send()
        for which in range(4):
            twin_right_of(which, m).wait_send()
        for source in range(2):
            act_beside_of(source, m).wait_send()
        e_twin(m).wait_send()
        e_beside(m).wait_send()
        e_onward(m).wait_send()
        grads_store(m).wait()

        @pl.when(jnp.logical_not(leads))
        def _(m=m):
            x_back(m).wait_send()

    @pl.loop(0, panels)
    def _(p):
        fin_of(p).wait_recv()

    @pl.loop(panels - RING, panels)
    def _(p):
        fin_of(p).wait_send()


def layers(tokens, cotangent, gains, biases, w_qkv, w_out, w_up, w_down):
    all_rows, width = tokens.shape
    hidden = w_up.shape[1]
    rows = all_rows // MICRO
    columns = 2 * hidden + 4 * width
    panels = columns // CORES // PANEL
    direct = hidden // CORES // PANEL
    pairs = panels - direct
    chunk = width // (LINE * PAIR)
    dma = pltpu.SemaphoreType.DMA
    shapes = {
        "h": ((all_rows, width), BF16),
        "e": ((all_rows, width), BF16),
        "result": ((all_rows, width), BF16),
        "w_qkv": (w_qkv.shape, BF16),
        "w_out": (w_out.shape, BF16),
        "w_up": (w_up.shape, BF16),
        "w_down": (w_down.shape, BF16),
        "left": ((3, CORES, all_rows, width), BF16),
        "e_half": ((4, all_rows, width // 2), BF16),
        "right": ((all_rows, columns), BF16),
        "twin_right": ((all_rows, columns // CORES), BF16),
        "act_beside": ((2, all_rows, hidden // CORES), BF16),
        "proj": ((all_rows, 3 * width), BF16),
        "middle": ((all_rows, width), F32),
        "up": ((all_rows, hidden), BF16),
        "probs": ((MICRO * HEADS, rows, rows), BF16),
        "bias": ((rows, rows), F32),
        "dctx": ((rows, width), BF16),
        "vector": ((8, width), F32),
        "parts": ((AHEAD, LINE, PAIR, chunk, PANEL), BF16),
        "acc": ((RING, LINE, chunk, PANEL), BF16),
        "fin": ((RING, chunk // 2, PANEL), F32),
        "pair_beside": ((2 * AHEAD, LINE, chunk, PANEL), BF16),
        "pair_in": ((RING, 3, chunk, PANEL), BF16),
        "pair_across": ((RING, 2, chunk, PANEL), BF16),
        "vectors": ((GROUP, 8, chunk), F32),
    }
    exchanges = {
        "x_forward": (MICRO,), "x_back": (MICRO,), "twin_left": (3, MICRO), "twin_right": (4, MICRO),
        "act_beside": (2, MICRO), "e_half": (3, MICRO), "pair_beside": (pairs,), "pair_in": (panels,),
        "pair_across": (panels,), "pair_out": (panels,), "fin": (panels,), "vector": (GROUP,),
    }
    semaphores = {"fetch": dma((5,)), "store": dma((2, MICRO))}
    for key, count in exchanges.items():
        semaphores[key + "_send"] = dma(count)
        semaphores[key + "_recv"] = dma(count)
    anywhere = pl.BlockSpec(memory_space=pl.ANY)
    in_vmem = pl.BlockSpec(memory_space=pltpu.VMEM)
    return pl.pallas_call(
        layer_kernel,
        out_shape=(
            jax.ShapeDtypeStruct((all_rows, width), BF16),
            jax.ShapeDtypeStruct((all_rows, width), BF16),
            jax.ShapeDtypeStruct((CORES, chunk // 2, columns // CORES), F32),
            jax.ShapeDtypeStruct((8, chunk), F32),
        ),
        in_specs=[anywhere] * 2 + [in_vmem] * 2 + [anywhere] * 4,
        out_specs=(anywhere, anywhere, in_vmem, in_vmem),
        scratch_shapes=[{key: pltpu.VMEM(*shape) for key, shape in shapes.items()}, semaphores],
        compiler_params=pltpu.CompilerParams(
            collective_id=1, has_side_effects=True, vmem_limit_bytes=64 * 2**20
        ),
        name="relay_layers",
    )(tokens, cotangent, gains, biases, w_qkv, w_out, w_up, w_down)


def reordered(member, axis, groups, back=False):
    shape = member.shape
    row = shape[axis] // (groups * GROUP)
    split = (GROUP, groups, row) if back else (groups, GROUP, row)
    apart = member.reshape(shape[:axis] + split + shape[axis + 1 :])
    return jnp.swapaxes(apart, axis, axis + 1).reshape(shape)


def on_device(tokens, cotangent, norm_gains, norm_biases, w_qkv, w_out, w_up, w_down):
    hidden, width = w_up.shape[2], tokens.shape[1]
    operands = (tokens, cotangent, norm_gains[0], norm_biases[0], w_qkv[0], w_out[0], w_up[0], w_down[0])
    groups = lax.axis_size("dp") // GROUP
    if groups > 1:
        axes = (1, 1, 1, 1, 0, 1, 0, 1)
        operands = tuple(reordered(member, axis, groups) for member, axis in zip(operands, axes))
    mixed, grads, block, vector_block = layers(*operands)
    core = lax.axis_index("dp") % CORES
    share = block.shape[1]
    vector_block = lax.dynamic_slice_in_dim(vector_block[:4], core * share, share, 1)
    pieces = []
    offset = 0
    for member in (hidden, hidden, width, 3 * width):
        half = member // CORES
        part = block[:, :, offset : offset + half]
        pieces.append(jnp.concatenate([part[0], part[1]], axis=1))
        offset += half
    if groups > 1:
        mixed, grads = (reordered(member, 1, groups, back=True) for member in (mixed, grads))
        same = [[g * GROUP + j for g in range(groups)] for j in range(GROUP)]

        def summed(member):
            return lax.psum_scatter(member, "dp", scatter_dimension=0, axis_index_groups=same, tiled=True)

        pieces = [summed(member) for member in pieces]
        vector_block = summed(vector_block.T).T
    down, up, out, qkv = pieces
    return (
        mixed[None], grads[None], qkv[None], out.T[None], up[None], down.T[None],
        vector_block[None, 0:2], vector_block[None, 2:4],
    )


def solution(mesh):
    placed = (P("dp", None),) * 2 + (P("section", None, None),) * 6
    return jax.shard_map(
        on_device,
        mesh=mesh,
        in_specs=placed,
        out_specs=(
            P("section", "dp", None),
            P("section", "dp", None),
            P("section", "dp", None),
            P("section", None, "dp"),
            P("section", "dp", None),
            P("section", None, "dp"),
            P("section", None, "dp"),
            P("section", None, "dp"),
        ),
        check_vma=False,
    )
```

time: 823 us -> 184 us (0.22); the launches traced: 815 us -> 184 us
  waiting for transfers between devices: 447 us -> 0 us
  matrix products: 258 us -> 0 us
  Pallas kernels: 0 us -> 175 us
  starting transfers between devices: 32.3 us -> 0 us
  other arithmetic: 29.7 us -> 2.69 us
  local copies, waits for them, and re-layouts: 30.9 us -> 5.59 us
  between operations: 17 us -> 0.71 us
    reduce_scatter x4 -> x0, waiting for transfers between devices: 416 us -> none  [the longest x1 140 us: on_device(): lax.psum_scatter(totals[2], 'dp', scatter_dimension=0, tiled=True)]
    dot_general x90 -> x0, matrix products: 258 us -> none  [the longest x5 47.9 us: backward(): jnp.einsum('rm,rn->mn', normed, grad_project, preferred_element_type=jnp....]
    pallas_call x0 -> x1, Pallas kernels: none -> 175 us  [layers(): pl.pallas_call(layer_kernel, out_shape=(jax.ShapeDtypeStruct((all_rows, w...]
    ppermute x10 -> x0, starting transfers between devices: 31.6 us -> none  [passed_along(): return lax.ppermute(block, axis, route)]
    ppermute x10 -> x0, waiting for transfers between devices: 30.5 us -> none  [passed_along(): return lax.ppermute(block, axis, route)]
    unnamed x314 -> x8, local copies, waits for them, and re-layouts: 21.3 us -> 1.9 us
    reduce_sum x25 -> x0, other arithmetic: 10.7 us -> none  [the longest x5 5.62 us: normalize(): average = jnp.mean(values, axis=-1, keepdims=True)]
  transfers between devices with their start and end apart: 16 -> 0, of which waited for: 13 -> 0; matrix products, arithmetic and copies ran while one was open for 19% -> 0% of each run, Pallas kernels for 0% -> 0%
where the time goes in v1:
time: 184 us
  Pallas kernels  175 us (95%)
  local copies, waits for them, and re-layouts  5.59 us (3%)
  other arithmetic  2.69 us (1%)
    pallas_call x1, Pallas kernels, layers(): pl.pallas_call(layer_kernel, out_shape=(jax.ShapeDtypeStruct((all_rows, w...  175 us

profile of v1, /device:TPU:0, one launch (start us, length us, event | category | flops | bytes accessed | tf_op | source)
XLA Modules:
  0.0 184.2 jit_solution(1577942495233185096)
XLA Ops:
  0.7 175.2 %relay_layers.1 = (bf16[480,1024]{1,0:T(8,128)(2,1)}, bf16[480,1024]{1,0:T(8,128)(2,1)}, f32[2,64,4096]{2,1,0:T(8,128)}, f32[8,128]{1,0:T(8,128)}) custom-call(bf16[480,1024]{1,0:T(8,128)(2,1)} %tokens_in.1, bf16[480,1024]{1,0:T(8,128)(2,1)} %cotangent_in.1, f32[2,1024]{1,0:T(2,128)} %bitcast.46, f32[2,1024]{1,0:T(2,128)} %bitcast.47, ...), custom_call_target="tpu_custom_call" | custom-call | tf_op jit(solution)/shard_map/relay_layers/pallas_call | solution.py:604
  175.8 0.0 copy-start
  175.8 0.8 slice.53
  176.7 0.1 constant_dynamic-slice_fusion
  176.7 0.6 slice_bitcast_fusion.8
  177.3 1.0 slice_bitcast_fusion.7
  178.3 0.7 maximum_bitcast_fusion.3
  179.0 1.2 slice_bitcast_fusion.1
  180.2 0.0 copy-done
  180.2 0.1 slice_bitcast_fusion.3
  180.3 0.0 copy-start.2
  180.3 0.9 maximum_bitcast_fusion
  181.2 0.0 copy-start.1
  181.2 1.0 maximum_bitcast_fusion.1
  182.3 0.0 copy-done.2
  182.3 0.9 copy.18
  183.2 0.0 copy-done.1
  183.2 0.9 copy.19
Async XLA Ops:
  175.8 4.4 %copy-start = (f32[2,64,4096]{2,1,0:T(8,128)S(1)}, f32[2,64,4096]{2,1,0:T(8,128)}, u32[]{:S(2)}) copy-start(f32[2,64,4096]{2,1,0:T(8,128)} %get-tuple-element.14) | copy-start | bytes 6291460
  180.3 2.0 %copy-start.2 = (bf16[480,1024]{1,0:T(8,128)(2,1)S(1)}, bf16[480,1024]{1,0:T(8,128)(2,1)}, u32[]{:S(2)}) copy-start(bf16[480,1024]{1,0:T(8,128)(2,1)} %get-tuple-element.12) | copy-start | bytes 2949124
  181.2 2.0 %copy-start.1 = (bf16[480,1024]{1,0:T(8,128)(2,1)S(1)}, bf16[480,1024]{1,0:T(8,128)(2,1)}, u32[]{:S(2)}) copy-start(bf16[480,1024]{1,0:T(8,128)(2,1)} %get-tuple-element.13) | copy-start | bytes 2949124

commit v2 on v1

--- a/solution.py
+++ b/solution.py
@@ -47,31 +47,22 @@
     return scale * (scaled - jnp.mean(scaled, axis=-1, keepdims=True) - unit * along)
 
 
-def gelu_parts(u):
+def gelu_and_slope(u):
     square = u * u
-    inner = jnp.tanh(0.7978845608 * u * (1.0 + 0.044715 * square))
-    return square, inner
-
-
-def gelu(u):
-    unused, inner = gelu_parts(u)
-    return 0.5 * u * (1.0 + inner)
-
-
-def gelu_slope(u):
-    square, inner = gelu_parts(u)
-    steep = 0.7978845608 * (1.0 + 3 * 0.044715 * square)
-    return 0.5 * (1.0 + inner) + 0.5 * u * (1.0 - inner * inner) * steep
+    inner = jnp.tanh(u * (0.7978845608 + 0.7978845608 * 0.044715 * square))
+    part = 0.5 + 0.5 * inner
+    steep = 0.5 * 0.7978845608 + 1.5 * 0.7978845608 * 0.044715 * square
+    return u * part, part + u * (1.0 - inner * inner) * steep
 
 
 def layer_kernel(
     tokens_in, cotangent_in, gains, biases, w_qkv_in, w_out_in, w_up_in, w_down_in,
     mixed_out, grads_out, out, vector_out, buf, sem,
 ):
-    h, e, result = buf["h"], buf["e"], buf["result"]
+    h, e, e_other, result = buf["h"], buf["e"], buf["e_other"], buf["result"]
     w_qkv, w_out, w_up, w_down = buf["w_qkv"], buf["w_out"], buf["w_up"], buf["w_down"]
     left, e_half, right, twin_right = buf["left"], buf["e_half"], buf["right"], buf["twin_right"]
-    act_beside, proj, middle, up = buf["act_beside"], buf["proj"], buf["middle"], buf["up"]
+    act_beside, proj, middle, slopes = buf["act_beside"], buf["proj"], buf["middle"], buf["slopes"]
     probs, bias, dctx, vector = buf["probs"], buf["bias"], buf["dctx"], buf["vector"]
     parts, acc, fin = buf["parts"], buf["acc"], buf["fin"]
     pair_beside, pair_in, pair_across = buf["pair_beside"], buf["pair_in"], buf["pair_across"]
@@ -79,6 +70,7 @@
 
     all_rows, width = h.shape
     rows = all_rows // MICRO
+    front = (rows // 2 + 15) // 16 * 16
     hidden = w_up.shape[1]
     chunk, half_chunk = acc.shape[2], acc.shape[2] // 2
     widths = (hidden, hidden, width, 3 * width)
@@ -124,19 +116,23 @@
     def rows_of(m):
         return pl.ds(pl.multiple_of(m * rows, rows), rows)
 
-    loads = [
-        fetch(w_qkv_in, w_qkv, 0), fetch(w_out_in, w_out, 1), fetch(w_up_in, w_up, 2), fetch(w_down_in, w_down, 3),
+    loads = [fetch(w_out_in, w_out, 0), fetch(w_up_in, w_up, 1), fetch(w_down_in, w_down, 2)]
+    loads_qkv = [
+        fetch(w_qkv_in.at[:, pl.ds(part * width, width)], w_qkv.at[:, pl.ds(part * width, width)], 3 + part)
+        for part in range(3)
     ]
+    load_rows = fetch(tokens_in, h, 6)
 
     @pl.when(leads)
     def _():
-        fetch(tokens_in, h, 4).start()
+        load_rows.start()
 
     @pl.when(jnp.logical_not(leads))
     def _():
-        fetch(cotangent_in, e, 4).start()
-
-    loads[0].start()
+        fetch(cotangent_in, e, 6).start()
+
+    for load in loads_qkv:
+        load.start()
     barrier = pltpu.get_barrier_semaphore()
     pl.semaphore_signal(barrier, inc=1, device_id=partner, device_id_type=MESH)
     for step in range(1, GROUP):
@@ -148,14 +144,15 @@
     seen = (row_ids // ITEM_LEN == col_ids // ITEM_LEN) & (col_ids <= row_ids)
     bias[...] = jnp.where(seen, 0.0, -1e30)
     vector[...] = jnp.zeros_like(vector)
+    proj[front:rows, width:] = jnp.zeros((rows - front, 2 * width), BF16)
     scale = 1.0 / math.sqrt(HEAD_DIM)
 
-    pl.semaphore_wait(barrier, GROUP)
-    fetch(tokens_in, h, 4).wait()
-
-
-    def x_forward(m):
-        return send(result.at[rows_of(m)], h.at[rows_of(m)], "x_forward", m, partner)
+
+    spans = ((0, front), (front, rows), (rows, 2 * rows))
+
+    def x_forward(i):
+        at = pl.ds(spans[i][0], spans[i][1] - spans[i][0])
+        return send(result.at[at], h.at[at], "x_forward", i, partner)
 
     def x_back(m):
         return send(h.at[rows_of(m)], e.at[rows_of(m)], "x_back", m, partner)
@@ -188,92 +185,98 @@
         return send(e_half.at[0, rows_of(m)], e_half.at[1, rows_of(m)], "e_half", (0, m), twin)
 
     def e_beside(m):
-        return send(result.at[rows_of(m), pl.ds(0, width // 2)], e_half.at[2, rows_of(m)], "e_half", (1, m), beside)
+        return send(e_other.at[rows_of(m)], e_half.at[2, rows_of(m)], "e_half", (1, m), beside)
 
     def e_onward(m):
         return send(e_half.at[2, rows_of(m)], e_half.at[3, rows_of(m)], "e_half", (2, m), twin)
 
 
-    def once(m, load, following=()):
-        @pl.when(m == 0)
-        def _():
-            loads[load].wait()
-            for other in following:
-                loads[other].start()
-
-    def forward(m):
-        at = rows_of(m)
+    def attend(i, load=False):
+        low, high = spans[i]
+        at, m = slice(low, high), low // rows
+        whole = slice(m * rows, (m + 1) * rows)
         unit, unused = normalized(h[at].astype(F32))
         left[QKV - 1, 0, at] = (unit * gains[0:1] + biases[0:1]).astype(BF16)
-        once(m, 0, (1, 2, 3))
         for part in range(3):
             cols = slice(part * width, (part + 1) * width)
+            if load:
+                loads_qkv[part].wait()
+                loads[part].start()
             proj[at, cols] = dot(left[QKV - 1, 0, at], w_qkv[:, cols]).astype(BF16)
-        twin_left(QKV, m).start()
-
-        @pl.loop(0, HEADS // 2)
-        def _(pair):
-            for member in range(2):
-                head = pair * 2 + member
-                q, k, v = (
-                    proj[at, pl.ds(pl.multiple_of(part * width + head * HEAD_DIM, HEAD_DIM), HEAD_DIM)]
-                    for part in range(3)
-                )
-                scores = dot_nt(q, k) * scale + bias[...]
-                weight = jnp.exp(scores - jnp.max(scores, axis=-1, keepdims=True))
-                weight = weight / jnp.sum(weight, axis=-1, keepdims=True)
-                weight = weight.astype(BF16)
-                probs[m * HEADS + head] = weight
-                cols = pl.ds(pl.multiple_of(columns_at[OUT] + head * HEAD_DIM, HEAD_DIM), HEAD_DIM)
-                right[at, cols] = dot(weight, v).astype(BF16)
-
-        once(m, 1)
-        twin_right_of(OUT, m).start()
+        for head in range(HEADS):
+            q, k, v = (proj[whole, part * width + head * HEAD_DIM : part * width + (head + 1) * HEAD_DIM] for part in range(3))
+            scores = dot_nt(q, k) * scale + bias[...]
+            weight = jnp.exp(scores - jnp.max(scores, axis=-1, keepdims=True))
+            weight = weight / jnp.sum(weight, axis=-1, keepdims=True)
+            weight = weight.astype(BF16)
+            probs[m * HEADS + head] = weight
+            cols = slice(columns_at[OUT] + head * HEAD_DIM, columns_at[OUT] + (head + 1) * HEAD_DIM)
+            right[whole, cols] = dot(weight, v).astype(BF16)
+
+    def forward(i, load=False):
+        at = slice(*spans[i])
+        if load:
+            loads[0].wait()
         attended = dot(right[at, columns_at[OUT] : columns_at[OUT] + width], w_out[...])
         middle[at] = h[at].astype(F32) + attended
         unit, unused = normalized(middle[at])
         left[UP - 1, 0, at] = (unit * gains[1:2] + biases[1:2]).astype(BF16)
-        twin_left(UP, m).start()
-        once(m, 2)
+        if load:
+            loads[1].wait()
         for part in range(2):
             cols = slice(part * hidden // 2, (part + 1) * hidden // 2)
             upward = dot(left[UP - 1, 0, at], w_up[:, cols])
-            up[at, cols] = upward.astype(BF16)
-            right[at, cols] = gelu(upward).astype(BF16)
+            active, slope = gelu_and_slope(upward)
+            slopes[at, cols] = slope.astype(BF16)
+            right[at, cols] = active.astype(BF16)
+        if load:
+            loads[2].wait()
+        result[at] = (middle[at] + dot(right[at, :hidden], w_down[...])).astype(BF16)
+
+        @pl.when(leads)
+        def _():
+            x_forward(i).start()
+
+    def share(m):
+        mixed_store(m).start()
         twin_right_of(DOWN, m).start()
         act_beside_of(0, m).start()
-        once(m, 3)
-        result[at] = (middle[at] + dot(right[at, :hidden], w_down[...])).astype(BF16)
-        mixed_store(m).start()
-
-        @pl.when(leads)
-        def _():
-            x_forward(m).start()
-
+        twin_right_of(OUT, m).start()
+        twin_left(QKV, m).start()
+        twin_left(UP, m).start()
+
+    def share_on(m):
         twin_right_of(DOWN, m).wait_recv()
         act_beside_of(1, m).start()
 
-    def backward(m, hook):
+    def spread(m):
         at = rows_of(m)
-        mixed_store(m).wait()
-
-        @pl.when(leads)
-        def _():
-            x_forward(m).wait_send()
-
         for zz in range(LINE):
             cols = pl.ds(zz * chunk, chunk)
             e_half[0, at, cols] = e[at, pl.ds(pl.multiple_of((zz * PAIR + y) * chunk, chunk), chunk)]
-            result[at, cols] = e[at, pl.ds(pl.multiple_of((zz * PAIR + other_y) * chunk, chunk), chunk)]
+            e_other[at, cols] = e[at, pl.ds(pl.multiple_of((zz * PAIR + other_y) * chunk, chunk), chunk)]
         e_beside(m).start()
         e_twin(m).start()
+
+    def backward(m, hook):
+        at = rows_of(m)
+
+        @pl.when(leads)
+        def _():
+            spread(m)
+
         for part in range(2):
             cols = slice(part * hidden // 2, (part + 1) * hidden // 2)
             passed = dot_nt(e[at], w_down[cols])
-            slope = gelu_slope(up[at, cols].astype(F32))
+            slope = slopes[at, cols].astype(F32)
             here = slice(columns_at[UP] + cols.start, columns_at[UP] + cols.stop)
             right[at, here] = (passed * slope).astype(BF16)
         twin_right_of(UP, m).start()
+
+        @pl.when(jnp.logical_not(leads))
+        def _():
+            share_on(m)
+
         grad = dot_nt(right[at, columns_at[UP] : columns_at[UP] + hidden], w_up[...])
         unit, size = normalized(middle[at])
         vector[1:2] += jnp.sum(grad * unit, axis=0, keepdims=True)
@@ -284,26 +287,20 @@
         dctx[...] = dot_nt(left[OUT - 1, 0, at], w_out[...]).astype(BF16)
         hook(m)
 
-        @pl.loop(0, HEADS // 2)
-        def _(pair):
-            for member in range(2):
-                head = pair * 2 + member
-                q, k, v = (
-                    proj[at, pl.ds(pl.multiple_of(part * width + head * HEAD_DIM, HEAD_DIM), HEAD_DIM)]
-                    for part in range(3)
-                )
-                grad_ctx = dctx[:, pl.ds(pl.multiple_of(head * HEAD_DIM, HEAD_DIM), HEAD_DIM)]
-                weight = probs[m * HEADS + head]
-                grad_weight = dot_nt(grad_ctx, v)
-                grad_v = dot_tn(weight, grad_ctx)
-                weight = weight.astype(F32)
-                total = jnp.sum(weight * grad_weight, axis=-1, keepdims=True)
-                grad_scores = (weight * (grad_weight - total)).astype(BF16)
-                grad_q = dot(grad_scores, k) * scale
-                grad_k = dot_tn(grad_scores, q) * scale
-                for part, value in enumerate((grad_q, grad_k, grad_v)):
-                    start = columns_at[QKV] + part * width + head * HEAD_DIM
-                    right[at, pl.ds(pl.multiple_of(start, HEAD_DIM), HEAD_DIM)] = value.astype(BF16)
+        for head in range(HEADS):
+            q, k, v = (proj[at, part * width + head * HEAD_DIM : part * width + (head + 1) * HEAD_DIM] for part in range(3))
+            grad_ctx = dctx[:, head * HEAD_DIM : (head + 1) * HEAD_DIM]
+            weight = probs[m * HEADS + head]
+            grad_weight = dot_nt(grad_ctx, v)
+            grad_v = dot_tn(weight, grad_ctx)
+            weight = weight.astype(F32)
+            total = jnp.sum(weight * grad_weight, axis=-1, keepdims=True)
+            grad_scores = (weight * (grad_weight - total)).astype(BF16)
+            grad_q = dot(grad_scores, k) * scale
+            grad_k = dot_tn(grad_scores, q) * scale
+            for part, value in enumerate((grad_q, grad_k, grad_v)):
+                start = columns_at[QKV] + part * width + head * HEAD_DIM
+                right[at, start : start + HEAD_DIM] = value.astype(BF16)
 
         twin_right_of(QKV, m).start()
         grad = dot_nt(right[at, columns_at[QKV] : columns_at[QKV] + 3 * width], w_qkv[...])
@@ -371,13 +368,14 @@
             parts[(p - direct) % AHEAD, numbered(zz)] = total[zz]
         beside_of(p).start()
 
-    def early():
+    def early_up():
         wait_for(UP)
 
         @pl.loop(direct, direct + AHEAD)
         def _(p):
             start_panel(p)
 
+    def early_down():
         for m in range(MICRO):
             e_beside(m).wait_recv()
             e_onward(m).start()
@@ -469,22 +467,58 @@
     def hook(m):
         @pl.when((m == MICRO - 1) & leads)
         def _():
-            early()
-
-    @pl.loop(0, 2 * MICRO)
+            early_up()
+            early_down()
+
+    @pl.when(leads)
+    def _():
+        load_rows.wait()
+        attend(0, load=True)
+
+    pl.semaphore_wait(barrier, GROUP)
+
+    @pl.when(jnp.logical_not(leads))
+    def _():
+        load_rows.wait()
+        for m in range(MICRO):
+            spread(m)
+        x_forward(0).wait_recv()
+        attend(0, load=True)
+
+    forward(0, load=True)
+
+    @pl.when(jnp.logical_not(leads))
+    def _():
+        x_forward(1).wait_recv()
+
+    attend(1)
+    forward(1)
+    share(0)
+
+    @pl.when(leads)
+    def _():
+        share_on(0)
+
+    @pl.loop(0, MICRO + 1)
     def _(step):
-        m = step % MICRO
-
-        @pl.when(step < MICRO)
+        @pl.when(step == section)
         def _():
             @pl.when(jnp.logical_not(leads))
             def _():
-                x_forward(m).wait_recv()
-
-            forward(m)
-
-        @pl.when(leads == (step >= MICRO))
-        def _():
+                x_forward(2).wait_recv()
+
+            attend(2)
+            forward(2)
+            share(1)
+
+            @pl.when(leads)
+            def _():
+                share_on(1)
+
+        @pl.when(step != section)
+        def _():
+            m = step // 2
+
             @pl.when(leads)
             def _():
                 x_back(m).wait_recv()
@@ -506,7 +540,8 @@
 
     @pl.when(jnp.logical_not(leads))
     def _():
-        early()
+        early_down()
+        early_up()
 
     @pl.loop(0, panels + 3)
     def _(t):
@@ -538,10 +573,16 @@
         e_beside(m).wait_send()
         e_onward(m).wait_send()
         grads_store(m).wait()
+        mixed_store(m).wait()
 
         @pl.when(jnp.logical_not(leads))
         def _(m=m):
             x_back(m).wait_send()
+
+    @pl.when(leads)
+    def _():
+        for i in range(len(spans)):
+            x_forward(i).wait_send()
 
     @pl.loop(0, panels)
     def _(p):
@@ -565,6 +606,7 @@
     shapes = {
         "h": ((all_rows, width), BF16),
         "e": ((all_rows, width), BF16),
+        "e_other": ((all_rows, width // 2), BF16),
         "result": ((all_rows, width), BF16),
         "w_qkv": (w_qkv.shape, BF16),
         "w_out": (w_out.shape, BF16),
@@ -577,7 +619,7 @@
         "act_beside": ((2, all_rows, hidden // CORES), BF16),
         "proj": ((all_rows, 3 * width), BF16),
         "middle": ((all_rows, width), F32),
-        "up": ((all_rows, hidden), BF16),
+        "slopes": ((all_rows, hidden), BF16),
         "probs": ((MICRO * HEADS, rows, rows), BF16),
         "bias": ((rows, rows), F32),
         "dctx": ((rows, width), BF16),
@@ -591,11 +633,11 @@
         "vectors": ((GROUP, 8, chunk), F32),
     }
     exchanges = {
-        "x_forward": (MICRO,), "x_back": (MICRO,), "twin_left": (3, MICRO), "twin_right": (4, MICRO),
+        "x_forward": (3,), "x_back": (MICRO,), "twin_left": (3, MICRO), "twin_right": (4, MICRO),
         "act_beside": (2, MICRO), "e_half": (3, MICRO), "pair_beside": (pairs,), "pair_in": (panels,),
         "pair_across": (panels,), "pair_out": (panels,), "fin": (panels,), "vector": (GROUP,),
     }
-    semaphores = {"fetch": dma((5,)), "store": dma((2, MICRO))}
+    semaphores = {"fetch": dma((7,)), "store": dma((2, MICRO))}
     for key, count in exchanges.items():
         semaphores[key + "_send"] = dma(count)
         semaphores[key + "_recv"] = dma(count)
@@ -619,6 +661,66 @@
     )(tokens, cotangent, gains, biases, w_qkv, w_out, w_up, w_down)
 
 
+def results_kernel(
+    mixed_in, grads_in, block_in, vectors_in, mixed, grads, down, up, out, qkv, gains, biases,
+    rows, block, vectors, shares, sem,
+):
+    started = []
+
+    def copy(source, target):
+        started.append(pltpu.make_async_copy(source, target, sem.at[len(started)]))
+        started[-1].start()
+        return started[-1]
+
+    fetches = [copy(block_in.at[core], block.at[core]) for core in range(CORES)]
+    fetches.append(copy(vectors_in, vectors))
+    fetches += [copy(ref, rows.at[i]) for i, ref in enumerate((mixed_in, grads_in))]
+    stores = []
+    for core in range(CORES):
+        fetches[core].wait()
+        offset = 0
+        for ref in (down, up, out, qkv):
+            half = ref.shape[1] // CORES
+            stores.append(copy(block.at[core, :, pl.ds(offset, half)], ref.at[:, pl.ds(core * half, half)]))
+            offset += half
+    fetches[CORES].wait()
+    share = gains.shape[1]
+    mine = lax.axis_index("dp") % CORES
+    for core in range(CORES):
+        @pl.when(mine == core)
+        def _(core=core):
+            here = slice(core * share, (core + 1) * share)
+            shares[0] = vectors[0:2, here]
+            shares[1] = vectors[2:4, here]
+
+    stores += [copy(shares.at[i], ref) for i, ref in enumerate((gains, biases))]
+    for i, ref in enumerate((mixed, grads)):
+        fetches[CORES + 1 + i].wait()
+        stores.append(copy(rows.at[i], ref))
+    for store in stores:
+        store.wait()
+
+
+def results(mixed, grads, block, vectors, hidden):
+    width, share = mixed.shape[1], block.shape[1]
+    anywhere = pl.BlockSpec(memory_space=pl.ANY)
+    shapes = ((share, hidden), (share, hidden), (share, width), (share, 3 * width), (2, share), (2, share))
+    mixed, grads, down, up, out, qkv, gains, biases = pl.pallas_call(
+        results_kernel,
+        out_shape=(jax.ShapeDtypeStruct(mixed.shape, BF16), jax.ShapeDtypeStruct(grads.shape, BF16))
+        + tuple(jax.ShapeDtypeStruct(shape, F32) for shape in shapes),
+        in_specs=[anywhere] * 4,
+        out_specs=(anywhere,) * 8,
+        scratch_shapes=[
+            pltpu.VMEM((2,) + mixed.shape, BF16), pltpu.VMEM(block.shape, F32), pltpu.VMEM(vectors.shape, F32),
+            pltpu.VMEM((2, 2, share), F32), pltpu.SemaphoreType.DMA((CORES + 3 + 4 * CORES + 4,)),
+        ],
+        compiler_params=pltpu.CompilerParams(vmem_limit_bytes=64 * 2**20),
+        name="place_results",
+    )(mixed, grads, block, vectors)
+    return mixed, grads, qkv, out.T, up, down.T, gains, biases
+
+
 def reordered(member, axis, groups, back=False):
     shape = member.shape
     row = shape[axis] // (groups * GROUP)
@@ -635,6 +737,8 @@
         axes = (1, 1, 1, 1, 0, 1, 0, 1)
         operands = tuple(reordered(member, axis, groups) for member, axis in zip(operands, axes))
     mixed, grads, block, vector_block = layers(*operands)
+    if groups == 1:
+        return tuple(member[None] for member in results(mixed, grads, block, vector_block, hidden))
     core = lax.axis_index("dp") % CORES
     share = block.shape[1]
     vector_block = lax.dynamic_slice_in_dim(vector_block[:4], core * share, share, 1)
@@ -645,15 +749,14 @@
         part = block[:, :, offset : offset + half]
         pieces.append(jnp.concatenate([part[0], part[1]], axis=1))
         offset += half
-    if groups > 1:
-        mixed, grads = (reordered(member, 1, groups, back=True) for member in (mixed, grads))
-        same = [[g * GROUP + j for g in range(groups)] for j in range(GROUP)]
-
-        def summed(member):
-            return lax.psum_scatter(member, "dp", scatter_dimension=0, axis_index_groups=same, tiled=True)
-
-        pieces = [summed(member) for member in pieces]
-        vector_block = summed(vector_block.T).T
+    mixed, grads = (reordered(member, 1, groups, back=True) for member in (mixed, grads))
+    same = [[g * GROUP + j for g in range(groups)] for j in range(GROUP)]
+
+    def summed(member):
+        return lax.psum_scatter(member, "dp", scatter_dimension=0, axis_index_groups=same, tiled=True)
+
+    pieces = [summed(member) for member in pieces]
+    vector_block = summed(vector_block.T).T
     down, up, out, qkv = pieces
     return (
         mixed[None], grads[None], qkv[None], out.T[None], up[None], down.T[None],

time: 184 us -> 165 us (0.90)
  Pallas kernels: 175 us -> 163 us
  local copies, waits for them, and re-layouts: 5.59 us -> 0 us
  other arithmetic: 2.69 us -> 0 us
    pallas_call x1, Pallas kernels: 175 us -> 160 us  [layers(): pl.pallas_call(layer_kernel, out_shape=(jax.ShapeDtypeStruct((all_rows, w...]
    pallas_call x0 -> x1, Pallas kernels: none -> 3.34 us  [results(): pl.pallas_call(results_kernel, out_shape=(jax.ShapeDtypeStruct(mixed.shap...]
    broadcast_in_dim x3 -> x0, other arithmetic: 2.69 us -> none  [the longest x1 1.04 us: on_device(): up[None]]
    squeeze x3 -> x0, local copies, waits for them, and re-layouts: 2.22 us -> none  [on_device(): pieces.append(jnp.concatenate([part[0], part[1]], axis=1))]
    unnamed x8 -> x0, local copies, waits for them, and re-layouts: 1.9 us -> none
where the time goes in v2:
time: 165 us; the launch traced here: 164 us
  Pallas kernels  163 us (99%)
    pallas_call x1, Pallas kernels, layers(): pl.pallas_call(layer_kernel, out_shape=(jax.ShapeDtypeStruct((all_rows, w...  160 us
    pallas_call x1, Pallas kernels, results(): pl.pallas_call(results_kernel, out_shape=(jax.ShapeDtypeStruct(mixed.shap...  3.34 us

profile of v2, /device:TPU:0, one launch (start us, length us, event | category | flops | bytes accessed | tf_op | source)
XLA Modules:
  0.0 164.0 jit_solution(6240460598811448664)
XLA Ops:
  0.6 159.8 %relay_layers.1 = (bf16[480,1024]{1,0:T(8,128)(2,1)}, bf16[480,1024]{1,0:T(8,128)(2,1)}, f32[2,64,4096]{2,1,0:T(8,128)}, f32[8,128]{1,0:T(8,128)}) custom-call(bf16[480,1024]{1,0:T(8,128)(2,1)} %tokens_in.1, bf16[480,1024]{1,0:T(8,128)(2,1)} %cotangent_in.1, f32[2,1024]{1,0:T(2,128)} %bitcast.22, f32[2,1024]{1,0:T(2,128)} %bitcast.23, ...), custom_call_target="tpu_custom_call" | custom-call | tf_op jit(solution)/shard_map/relay_layers/pallas_call | solution.py:646
  160.5 3.3 %place_results.1 = (bf16[480,1024]{1,0:T(8,128)(2,1)}, bf16[480,1024]{1,0:T(8,128)(2,1)}, f32[64,2048]{1,0:T(8,128)}, f32[64,2048]{1,0:T(8,128)}, f32[64,1024]{1...) custom-call(bf16[480,1024]{1,0:T(8,128)(2,1)} %get-tuple-element.20.mixed_in, ...), custom_call_target="tpu_custom_call" | custom-call | tf_op jit(solution)/shard_map/place_results/pallas_call | solution.py:708

commit v3 on v2

--- a/solution.py
+++ b/solution.py
@@ -16,8 +16,13 @@
 LINE, PAIR, CORES = 4, 2, 2
 GROUP = LINE * PAIR * CORES
 PANEL = 256
-AHEAD = 4
-RING = 4
+STRIPS = 2
+AHEAD = 8
+LAG = 2
+BEFORE_HEADS, BEFORE_LAST = 4, 5
+RING = 8
+FIRST = 4
+LEAVING = 8
 MESH = pl.DeviceIdType.MESH
 BF16, F32 = jnp.bfloat16, jnp.float32
 DOWN, UP, OUT, QKV = range(4)
@@ -78,7 +83,8 @@
     starts = [0]
     for member in widths:
         starts.append(starts[-1] + member // CORES // PANEL)
-    panels, direct = starts[-1], starts[1]
+    strip = PANEL // STRIPS
+    strips, direct = starts[-1] * STRIPS, starts[1] * STRIPS
     halves = [member // CORES for member in widths]
     twin_at = [start * PANEL for start in starts]
 
@@ -104,10 +110,10 @@
     partner = (1 - section, place)
     leads = section == 0
 
-    def send(source, target, key, index, to):
+    def send(source, target, key, index, to, landing=None):
         return pltpu.make_async_remote_copy(
             src_ref=source, dst_ref=target, send_sem=sem[key + "_send"].at[index],
-            recv_sem=sem[key + "_recv"].at[index], device_id=to, device_id_type=MESH,
+            recv_sem=sem[key + "_recv"].at[index if landing is None else landing], device_id=to, device_id_type=MESH,
         )
 
     def fetch(source, target, index):
@@ -131,14 +137,14 @@
     def _():
         fetch(cotangent_in, e, 6).start()
 
-    for load in loads_qkv:
-        load.start()
     barrier = pltpu.get_barrier_semaphore()
     pl.semaphore_signal(barrier, inc=1, device_id=partner, device_id_type=MESH)
     for step in range(1, GROUP):
         peer = (section, first + (mine + step) % GROUP)
         pl.semaphore_signal(barrier, inc=1, device_id=peer, device_id_type=MESH)
 
+    for load in loads_qkv:
+        load.start()
     row_ids = lax.broadcasted_iota(jnp.int32, (rows, rows), 0)
     col_ids = lax.broadcasted_iota(jnp.int32, (rows, rows), 1)
     seen = (row_ids // ITEM_LEN == col_ids // ITEM_LEN) & (col_ids <= row_ids)
@@ -154,8 +160,13 @@
         at = pl.ds(spans[i][0], spans[i][1] - spans[i][0])
         return send(result.at[at], h.at[at], "x_forward", i, partner)
 
-    def x_back(m):
-        return send(h.at[rows_of(m)], e.at[rows_of(m)], "x_back", m, partner)
+    returns = ((0, rows), (rows, rows + front), (rows + front, 2 * rows))
+
+    def returned(i):
+        return pl.ds(returns[i][0], returns[i][1] - returns[i][0])
+
+    def x_back(i):
+        return send(h.at[returned(i)], e.at[returned(i)], "x_back", i, partner)
 
     def mixed_store(m):
         return pltpu.make_async_copy(result.at[rows_of(m)], mixed_out.at[rows_of(m)], sem["store"].at[0, m])
@@ -173,22 +184,20 @@
                     twin_right.at[rows_of(m), pl.ds(twin_at[which], halves[which])],
                     "twin_right", (which, m), twin)
 
-    def act_beside_of(source, m):
-        if source == 0:
-            start = pl.multiple_of(core * halves[DOWN], 128)
-            held = right.at[rows_of(m), pl.ds(start, halves[DOWN])]
-        else:
-            held = twin_right.at[rows_of(m), pl.ds(0, halves[DOWN])]
-        return send(held, act_beside.at[source, rows_of(m)], "act_beside", (source, m), beside)
-
-    def e_twin(m):
-        return send(e_half.at[0, rows_of(m)], e_half.at[1, rows_of(m)], "e_half", (0, m), twin)
-
-    def e_beside(m):
-        return send(e_other.at[rows_of(m)], e_half.at[2, rows_of(m)], "e_half", (1, m), beside)
-
-    def e_onward(m):
-        return send(e_half.at[2, rows_of(m)], e_half.at[3, rows_of(m)], "e_half", (2, m), twin)
+    def a2_beside(m):
+        return send(left.at[UP - 1, 0, rows_of(m)], act_beside.at[0, rows_of(m)], "act_beside", (0, m), beside)
+
+    def a2_onward(m):
+        return send(act_beside.at[0, rows_of(m)], act_beside.at[1, rows_of(m)], "act_beside", (1, m), twin)
+
+    def e_twin(i):
+        return send(e_half.at[0, returned(i)], e_half.at[1, returned(i)], "e_half", (0, i), twin)
+
+    def e_beside(i):
+        return send(e_other.at[returned(i)], e_half.at[2, returned(i)], "e_half", (1, i), beside)
+
+    def e_onward(i):
+        return send(e_half.at[2, returned(i)], e_half.at[3, returned(i)], "e_half", (2, i), twin)
 
 
     def attend(i, load=False):
@@ -221,6 +230,8 @@
         middle[at] = h[at].astype(F32) + attended
         unit, unused = normalized(middle[at])
         left[UP - 1, 0, at] = (unit * gains[1:2] + biases[1:2]).astype(BF16)
+        if i > 0:
+            a2_beside(i - 1).start()
         if load:
             loads[1].wait()
         for part in range(2):
@@ -240,30 +251,35 @@
     def share(m):
         mixed_store(m).start()
         twin_right_of(DOWN, m).start()
-        act_beside_of(0, m).start()
         twin_right_of(OUT, m).start()
         twin_left(QKV, m).start()
         twin_left(UP, m).start()
 
-    def share_on(m):
-        twin_right_of(DOWN, m).wait_recv()
-        act_beside_of(1, m).start()
-
-    def spread(m):
-        at = rows_of(m)
+    def gather_act():
+        cols = pl.ds(pl.multiple_of(core * halves[DOWN], 128), halves[DOWN])
+
+        @pl.loop(0, MICRO)
+        def _(m):
+            a2_beside(m).wait_recv()
+            a2_onward(m).start()
+            a2_onward(m).wait()
+
+            @pl.loop(0, 2)
+            def _(source):
+                active, unused = gelu_and_slope(dot(act_beside[source, rows_of(m)], w_up[:, cols]))
+                act_beside[source, rows_of(m)] = active.astype(BF16)
+
+    def spread(i):
+        at = returned(i)
         for zz in range(LINE):
             cols = pl.ds(zz * chunk, chunk)
             e_half[0, at, cols] = e[at, pl.ds(pl.multiple_of((zz * PAIR + y) * chunk, chunk), chunk)]
             e_other[at, cols] = e[at, pl.ds(pl.multiple_of((zz * PAIR + other_y) * chunk, chunk), chunk)]
-        e_beside(m).start()
-        e_twin(m).start()
-
-    def backward(m, hook):
+        e_beside(i).start()
+        e_twin(i).start()
+
+    def backward(m, hooks):
         at = rows_of(m)
-
-        @pl.when(leads)
-        def _():
-            spread(m)
 
         for part in range(2):
             cols = slice(part * hidden // 2, (part + 1) * hidden // 2)
@@ -273,10 +289,7 @@
             right[at, here] = (passed * slope).astype(BF16)
         twin_right_of(UP, m).start()
 
-        @pl.when(jnp.logical_not(leads))
-        def _():
-            share_on(m)
-
+        hooks[0](m)
         grad = dot_nt(right[at, columns_at[UP] : columns_at[UP] + hidden], w_up[...])
         unit, size = normalized(middle[at])
         vector[1:2] += jnp.sum(grad * unit, axis=0, keepdims=True)
@@ -285,7 +298,7 @@
         left[OUT - 1, 0, at] = middle[at].astype(BF16)
         twin_left(OUT, m).start()
         dctx[...] = dot_nt(left[OUT - 1, 0, at], w_out[...]).astype(BF16)
-        hook(m)
+        hooks[1](m)
 
         for head in range(HEADS):
             q, k, v = (proj[at, part * width + head * HEAD_DIM : part * width + (head + 1) * HEAD_DIM] for part in range(3))
@@ -303,6 +316,7 @@
                 right[at, start : start + HEAD_DIM] = value.astype(BF16)
 
         twin_right_of(QKV, m).start()
+        hooks[2](m)
         grad = dot_nt(right[at, columns_at[QKV] : columns_at[QKV] + 3 * width], w_qkv[...])
         unit, size = normalized(h[at].astype(F32))
         vector[0:1] += jnp.sum(grad * unit, axis=0, keepdims=True)
@@ -312,24 +326,35 @@
 
         @pl.when(jnp.logical_not(leads))
         def _():
-            x_back(m).start()
+            @pl.when(m == 0)
+            def _():
+                x_back(0).start()
+
+            @pl.when(m == 1)
+            def _():
+                x_back(1).start()
 
 
     def beside_of(p):
         i = p - direct
-        return send(parts.at[i % AHEAD, :, other_y], pair_beside.at[i % (2 * AHEAD)], "pair_beside", i, beside)
+        here, there = i % AHEAD, i % (2 * AHEAD)
+        return send(parts.at[here, :, other_y], pair_beside.at[there], "pair_beside", here, beside, there)
 
     def in_of(p):
-        return send(acc.at[p % RING, pl.ds(1, 3)], pair_in.at[p % RING], "pair_in", p, inner)
+        return send(acc.at[p % RING, pl.ds(1, 3)], pair_in.at[p % RING], "pair_in", p % RING, inner)
 
     def across_of(p):
-        return send(acc.at[p % RING, pl.ds(2, 2)], pair_across.at[p % RING], "pair_across", p, across)
+        return send(acc.at[p % RING, pl.ds(2, 2)], pair_across.at[p % RING], "pair_across", p % RING, across)
 
     def out_of(p):
-        return send(acc.at[p % RING, 0], pair_in.at[p % RING, 0], "pair_out", p, end)
-
-    def fin_of(p):
-        return send(fin.at[p % RING], out.at[core, :, pl.ds(pl.multiple_of(p * PANEL, PANEL), PANEL)], "fin", p, twin)
+        return send(acc.at[p % RING, 0], pair_in.at[p % RING, 0], "pair_out", p % RING, end)
+
+    def strip_columns(p):
+        return pl.ds(pl.multiple_of(p * strip, strip), strip)
+
+    def fin_of(g):
+        cols = pl.ds(pl.multiple_of(g * LEAVING * strip, LEAVING * strip), LEAVING * strip)
+        return send(fin.at[:, cols], out.at[core, :, cols], "fin", g, twin)
 
     def add(target, *refs):
         total = target[...].astype(F32)
@@ -353,7 +378,7 @@
             twin_left(which, m).wait_recv()
             twin_right_of(which, m).wait_recv()
 
-    def start_panel(p):
+    def form(p):
         which = 0
         for i in (OUT, QKV):
             which = which + (p >= starts[i]).astype(jnp.int32)
@@ -363,47 +388,55 @@
                 wait_for(i)
 
         total = dot_tn(left[which, 0], right[:, own_columns(p)]) + dot_tn(left[which, 1], twin_right[:, twin_columns(p)])
-        total = total.astype(BF16).reshape(parts.shape[1:])
-        for zz in range(LINE):
-            parts[(p - direct) % AHEAD, numbered(zz)] = total[zz]
-        beside_of(p).start()
-
-    def early_up():
-        wait_for(UP)
-
-        @pl.loop(direct, direct + AHEAD)
+        total = total.astype(BF16).reshape(LINE, PAIR, chunk, PANEL)
+        for part in range(STRIPS):
+            for zz in range(LINE):
+                here = total[zz, :, :, part * strip : (part + 1) * strip]
+                parts[(p * STRIPS + part - direct) % AHEAD, numbered(zz)] = here
+
+    def form_up(low, high):
+        @pl.loop(starts[UP] + low, starts[UP] + high)
         def _(p):
-            start_panel(p)
-
-    def early_down():
+            form(p)
+
+    def start_strips(low, high):
+        @pl.loop(direct + low, direct + high)
+        def _(p):
+            beside_of(p).start()
+
+    def gather_e(i):
+        e_beside(i).wait_recv()
+        e_onward(i).start()
+
+    def form_down():
         for m in range(MICRO):
-            e_beside(m).wait_recv()
-            e_onward(m).start()
-        for m in range(MICRO):
-            e_twin(m).wait_recv()
-            act_beside_of(0, m).wait_recv()
-            act_beside_of(1, m).wait_recv()
-            e_onward(m).wait_recv()
-
-        @pl.loop(0, direct)
+            twin_right_of(DOWN, m).wait_recv()
+        for i in range(len(returns)):
+            e_twin(i).wait_recv()
+            e_onward(i).wait_recv()
+
+        @pl.loop(0, starts[UP])
         def _(p):
             total = dot_tn(e_half[0], right[:, own_columns(p)]) + dot_tn(e_half[1], twin_right[:, twin_columns(p)])
             for source in range(2):
                 total = total + dot_tn(e_half[2 + source], act_beside[source, :, twin_columns(p)])
-            total = total.astype(BF16).reshape(acc.shape[1:])
-            for zz in range(LINE):
-                acc[p % RING, numbered(zz)] = total[zz]
-
-            @pl.when(is_end & (p < 2))
-            def _():
-                in_of(p).start()
-
-    def proceed(t):
-        @pl.when((t < direct - 2) & is_end)
-        def _():
-            in_of(t + 2).start()
-
-        @pl.when((t >= direct) & (t < panels))
+            total = total.astype(BF16).reshape(LINE, chunk, PANEL)
+            for part in range(STRIPS):
+                for zz in range(LINE):
+                    acc[(p * STRIPS + part) % RING, numbered(zz)] = total[zz, :, part * strip : (part + 1) * strip]
+
+            @pl.when(is_end & (p < FIRST // STRIPS))
+            def _():
+                for part in range(STRIPS):
+                    in_of(p * STRIPS + part).start()
+
+    def enter(t):
+        @pl.when((t < direct - FIRST) & is_end)
+        def _():
+            in_of(t + FIRST).start()
+
+    def across_y(t):
+        @pl.when((t >= direct) & (t < strips))
         def _():
             i = t - direct
             beside_of(t).wait()
@@ -415,29 +448,34 @@
             def _():
                 in_of(t).start()
 
-            @pl.when(t + AHEAD < panels)
-            def _():
-                start_panel(t + AHEAD)
-
-        p = t - 1
-
-        @pl.when((p >= 0) & (p < panels) & is_inner)
+            @pl.when(t + AHEAD < strips)
+            def _():
+                @pl.when(t % STRIPS == STRIPS - 1)
+                def _():
+                    form((t + AHEAD) // STRIPS)
+                    for part in range(STRIPS):
+                        beside_of(t + AHEAD - STRIPS + 1 + part).start()
+
+    def relay(t):
+        p = t - LAG
+
+        @pl.when((p >= 0) & (p < strips) & is_inner)
         def _():
             in_of(p).wait_recv()
             add(acc.at[p % RING, pl.ds(2, 2)], pair_in.at[p % RING, pl.ds(1, 2)])
             across_of(p).start()
             add(acc.at[p % RING, 1], pair_in.at[p % RING, 0])
 
-        q = t - 2
-
-        @pl.when((q >= 0) & (q < panels) & is_inner)
+        q = t - 2 * LAG
+
+        @pl.when((q >= 0) & (q < strips) & is_inner)
         def _():
             across_of(q).wait_recv()
             add(acc.at[q % RING, 0], pair_across.at[q % RING, 1])
             out_of(q).start()
             add(acc.at[q % RING, 1], pair_across.at[q % RING, 0])
 
-        r = t - 3
+        r = t - 3 * LAG
 
         @pl.when(r >= 0)
         def _():
@@ -455,20 +493,42 @@
             def block(which):
                 return acc[r % RING, own, pl.ds(pl.multiple_of(which * half_chunk, half_chunk), half_chunk)].astype(F32)
 
-            @pl.when(r >= RING)
-            def _():
-                fin_of(r - RING).wait_send()
-
-            fin[r % RING] = block(other_core)
-            fin_of(r).start()
-            out[core, :, twin_columns(r)] = block(core)
-
-
-    def hook(m):
+            out[core, :, strip_columns(r)] = block(core)
+            fin[:, strip_columns(r)] = block(other_core)
+
+            @pl.when(r % LEAVING == LEAVING - 1)
+            def _():
+                fin_of(r // LEAVING).start()
+
+    def proceed(low, high, parts_of_step):
+        @pl.loop(low, high)
+        def _(t):
+            for part in parts_of_step:
+                part(t)
+
+
+    def after_du(m):
         @pl.when((m == MICRO - 1) & leads)
         def _():
-            early_up()
-            early_down()
+            for i in range(2):
+                gather_e(i)
+            wait_for(UP)
+            form_up(0, 2)
+            start_strips(0, 2 * STRIPS)
+            gather_e(2)
+            form_down()
+
+    def after_middle(m):
+        @pl.when((m == MICRO - 1) & leads)
+        def _():
+            form_up(2, AHEAD // STRIPS)
+            start_strips(2 * STRIPS, AHEAD)
+            proceed(0, BEFORE_HEADS, (enter, relay))
+
+    def after_heads(m):
+        @pl.when((m == MICRO - 1) & leads)
+        def _():
+            proceed(BEFORE_HEADS, BEFORE_LAST, (enter, relay))
 
     @pl.when(leads)
     def _():
@@ -480,8 +540,8 @@
     @pl.when(jnp.logical_not(leads))
     def _():
         load_rows.wait()
-        for m in range(MICRO):
-            spread(m)
+        for i in range(len(returns)):
+            spread(i)
         x_forward(0).wait_recv()
         attend(0, load=True)
 
@@ -495,10 +555,6 @@
     forward(1)
     share(0)
 
-    @pl.when(leads)
-    def _():
-        share_on(0)
-
     @pl.loop(0, MICRO + 1)
     def _(step):
         @pl.when(step == section)
@@ -513,17 +569,24 @@
 
             @pl.when(leads)
             def _():
-                share_on(1)
+                gather_act()
 
         @pl.when(step != section)
         def _():
             m = step // 2
 
-            @pl.when(leads)
-            def _():
-                x_back(m).wait_recv()
-
-            backward(m, hook)
+            @pl.when(leads & (m == 0))
+            def _():
+                x_back(0).wait_recv()
+                spread(0)
+
+            @pl.when(leads & (m == 1))
+            def _():
+                for i in (1, 2):
+                    x_back(i).wait_recv()
+                    spread(i)
+
+            backward(m, (after_du, after_middle, after_heads))
 
     def send_vector(step):
         peer = (mine + step) % GROUP
@@ -540,12 +603,18 @@
 
     @pl.when(jnp.logical_not(leads))
     def _():
-        early_down()
-        early_up()
-
-    @pl.loop(0, panels + 3)
-    def _(t):
-        proceed(t)
+        wait_for(UP)
+        form_up(0, AHEAD // STRIPS)
+        x_back(2).start()
+        start_strips(0, AHEAD)
+        for i in range(len(returns)):
+            gather_e(i)
+        gather_act()
+        form_down()
+
+        proceed(0, BEFORE_LAST, (enter, relay))
+
+    proceed(BEFORE_LAST, strips + 3 * LAG, (enter, across_y, relay))
 
     vector_total = vector[:, pl.ds(pl.multiple_of((mine // CORES) * chunk, chunk), chunk)]
     for step in range(1, GROUP):
@@ -567,30 +636,28 @@
             twin_left(which, m).wait_send()
         for which in range(4):
             twin_right_of(which, m).wait_send()
-        for source in range(2):
-            act_beside_of(source, m).wait_send()
-        e_twin(m).wait_send()
-        e_beside(m).wait_send()
-        e_onward(m).wait_send()
+        a2_beside(m).wait_send()
         grads_store(m).wait()
         mixed_store(m).wait()
 
-        @pl.when(jnp.logical_not(leads))
-        def _(m=m):
-            x_back(m).wait_send()
+    for i in range(len(returns)):
+        e_twin(i).wait_send()
+        e_beside(i).wait_send()
+        e_onward(i).wait_send()
+
+    @pl.when(jnp.logical_not(leads))
+    def _():
+        for i in range(len(returns)):
+            x_back(i).wait_send()
 
     @pl.when(leads)
     def _():
         for i in range(len(spans)):
             x_forward(i).wait_send()
 
-    @pl.loop(0, panels)
-    def _(p):
-        fin_of(p).wait_recv()
-
-    @pl.loop(panels - RING, panels)
-    def _(p):
-        fin_of(p).wait_send()
+    @pl.loop(0, strips // LEAVING)
+    def _(g):
+        fin_of(g).wait()
 
 
 def layers(tokens, cotangent, gains, biases, w_qkv, w_out, w_up, w_down):
@@ -598,9 +665,8 @@
     hidden = w_up.shape[1]
     rows = all_rows // MICRO
     columns = 2 * hidden + 4 * width
-    panels = columns // CORES // PANEL
-    direct = hidden // CORES // PANEL
-    pairs = panels - direct
+    strip = PANEL // STRIPS
+    strips = columns // CORES // strip
     chunk = width // (LINE * PAIR)
     dma = pltpu.SemaphoreType.DMA
     shapes = {
@@ -624,23 +690,24 @@
         "bias": ((rows, rows), F32),
         "dctx": ((rows, width), BF16),
         "vector": ((8, width), F32),
-        "parts": ((AHEAD, LINE, PAIR, chunk, PANEL), BF16),
-        "acc": ((RING, LINE, chunk, PANEL), BF16),
-        "fin": ((RING, chunk // 2, PANEL), F32),
-        "pair_beside": ((2 * AHEAD, LINE, chunk, PANEL), BF16),
-        "pair_in": ((RING, 3, chunk, PANEL), BF16),
-        "pair_across": ((RING, 2, chunk, PANEL), BF16),
+        "parts": ((AHEAD, LINE, PAIR, chunk, strip), BF16),
+        "acc": ((RING, LINE, chunk, strip), BF16),
+        "fin": ((chunk // 2, columns // CORES), F32),
+        "pair_beside": ((2 * AHEAD, LINE, chunk, strip), BF16),
+        "pair_in": ((RING, 3, chunk, strip), BF16),
+        "pair_across": ((RING, 2, chunk, strip), BF16),
         "vectors": ((GROUP, 8, chunk), F32),
     }
     exchanges = {
-        "x_forward": (3,), "x_back": (MICRO,), "twin_left": (3, MICRO), "twin_right": (4, MICRO),
-        "act_beside": (2, MICRO), "e_half": (3, MICRO), "pair_beside": (pairs,), "pair_in": (panels,),
-        "pair_across": (panels,), "pair_out": (panels,), "fin": (panels,), "vector": (GROUP,),
+        "x_forward": (3,), "x_back": (3,), "twin_left": (3, MICRO), "twin_right": (4, MICRO),
+        "act_beside": (2, MICRO), "e_half": (3, 3), "pair_in": (RING,), "pair_across": (RING,), "pair_out": (RING,),
+        "fin": (strips // LEAVING,), "vector": (GROUP,),
     }
     semaphores = {"fetch": dma((7,)), "store": dma((2, MICRO))}
     for key, count in exchanges.items():
         semaphores[key + "_send"] = dma(count)
         semaphores[key + "_recv"] = dma(count)
+    semaphores["pair_beside_send"], semaphores["pair_beside_recv"] = dma((AHEAD,)), dma((2 * AHEAD,))
     anywhere = pl.BlockSpec(memory_space=pl.ANY)
     in_vmem = pl.BlockSpec(memory_space=pltpu.VMEM)
     return pl.pallas_call(

time: 165 us -> 158 us (0.958)
  Pallas kernels: 163 us -> 157 us
    pallas_call x1, Pallas kernels: 160 us -> 154 us  [layers(): pl.pallas_call(layer_kernel, out_shape=(jax.ShapeDtypeStruct((all_rows, w...]
where the time goes in v3:
time: 158 us
  Pallas kernels  157 us (99%)
    pallas_call x1, Pallas kernels, layers(): pl.pallas_call(layer_kernel, out_shape=(jax.ShapeDtypeStruct((all_rows, w...  154 us
    pallas_call x1, Pallas kernels, results(): pl.pallas_call(results_kernel, out_shape=(jax.ShapeDtypeStruct(mixed.shap...  3.34 us

profile of v3, /device:TPU:0, one launch (start us, length us, event | category | flops | bytes accessed | tf_op | source)
XLA Modules:
  0.0 157.8 jit_solution(14749539231436169256)
XLA Ops:
  0.6 153.6 %relay_layers.1 = (bf16[480,1024]{1,0:T(8,128)(2,1)}, bf16[480,1024]{1,0:T(8,128)(2,1)}, f32[2,64,4096]{2,1,0:T(8,128)}, f32[8,128]{1,0:T(8,128)}) custom-call(bf16[480,1024]{1,0:T(8,128)(2,1)} %tokens_in.1, bf16[480,1024]{1,0:T(8,128)(2,1)} %cotangent_in.1, f32[2,1024]{1,0:T(2,128)} %bitcast.22, f32[2,1024]{1,0:T(2,128)} %bitcast.23, ...), custom_call_target="tpu_custom_call" | custom-call | tf_op jit(solution)/shard_map/relay_layers/pallas_call | solution.py:713
  154.3 3.3 %place_results.1 = (bf16[480,1024]{1,0:T(8,128)(2,1)}, bf16[480,1024]{1,0:T(8,128)(2,1)}, f32[64,2048]{1,0:T(8,128)}, f32[64,2048]{1,0:T(8,128)}, f32[64,1024]{1...) custom-call(bf16[480,1024]{1,0:T(8,128)(2,1)} %get-tuple-element.20.mixed_in, ...), custom_call_target="tpu_custom_call" | custom-call | tf_op jit(solution)/shard_map/place_results/pallas_call | solution.py:775

commit v4 on v3

--- a/solution.py
+++ b/solution.py
@@ -17,10 +17,13 @@
 GROUP = LINE * PAIR * CORES
 PANEL = 256
 STRIPS = 2
-AHEAD = 8
+AHEAD = 10
 LAG = 2
+END_LAG = 5
 BEFORE_HEADS, BEFORE_LAST = 4, 5
 RING = 8
+END_RING = 12
+VECTORS = 8, 22
 FIRST = 4
 LEAVING = 8
 MESH = pl.DeviceIdType.MESH
@@ -71,7 +74,7 @@
     probs, bias, dctx, vector = buf["probs"], buf["bias"], buf["dctx"], buf["vector"]
     parts, acc, fin = buf["parts"], buf["acc"], buf["fin"]
     pair_beside, pair_in, pair_across = buf["pair_beside"], buf["pair_in"], buf["pair_across"]
-    vectors = buf["vectors"]
+    vectors, vectors_line = buf["vectors"], buf["vectors_line"]
 
     all_rows, width = h.shape
     rows = all_rows // MICRO
@@ -105,7 +108,6 @@
     def device(zz, yy, cc):
         return (section, first + (zz * PAIR + yy) * CORES + cc)
 
-    inner, end, across = (device(numbered(zz), y, core) for zz in (1, 0, 2))
     beside, twin = device(z, other_y, core), device(z, y, other_core)
     partner = (1 - section, place)
     leads = section == 0
@@ -138,11 +140,11 @@
         fetch(cotangent_in, e, 6).start()
 
     barrier = pltpu.get_barrier_semaphore()
-    pl.semaphore_signal(barrier, inc=1, device_id=partner, device_id_type=MESH)
-    for step in range(1, GROUP):
-        peer = (section, first + (mine + step) % GROUP)
+    lined = [device((z + step) % LINE, y, core) for step in range(1, LINE)]
+    inner, end, across, far_end = (device(numbered(zz), y, core) for zz in (1, 0, 2, 3))
+    peers = [partner, twin, beside] + lined
+    for peer in peers:
         pl.semaphore_signal(barrier, inc=1, device_id=peer, device_id_type=MESH)
-
     for load in loads_qkv:
         load.start()
     row_ids = lax.broadcasted_iota(jnp.int32, (rows, rows), 0)
@@ -160,7 +162,8 @@
         at = pl.ds(spans[i][0], spans[i][1] - spans[i][0])
         return send(result.at[at], h.at[at], "x_forward", i, partner)
 
-    returns = ((0, rows), (rows, rows + front), (rows + front, 2 * rows))
+    late = rows // 5
+    returns = ((0, rows), (rows, rows + front), (rows + front, 2 * rows - late), (2 * rows - late, 2 * rows))
 
     def returned(i):
         return pl.ds(returns[i][0], returns[i][1] - returns[i][0])
@@ -212,15 +215,17 @@
                 loads_qkv[part].wait()
                 loads[part].start()
             proj[at, cols] = dot(left[QKV - 1, 0, at], w_qkv[:, cols]).astype(BF16)
+        def heads_of(part, head):
+            start = part * width + head * HEAD_DIM
+            return proj[whole, start : start + HEAD_DIM]
+
         for head in range(HEADS):
-            q, k, v = (proj[whole, part * width + head * HEAD_DIM : part * width + (head + 1) * HEAD_DIM] for part in range(3))
-            scores = dot_nt(q, k) * scale + bias[...]
+            scores = dot_nt(heads_of(0, head), heads_of(1, head)) * scale + bias[...]
             weight = jnp.exp(scores - jnp.max(scores, axis=-1, keepdims=True))
-            weight = weight / jnp.sum(weight, axis=-1, keepdims=True)
-            weight = weight.astype(BF16)
-            probs[m * HEADS + head] = weight
+            probs[m * HEADS + head] = (weight / jnp.sum(weight, axis=-1, keepdims=True)).astype(BF16)
+        for head in range(HEADS):
             cols = slice(columns_at[OUT] + head * HEAD_DIM, columns_at[OUT] + (head + 1) * HEAD_DIM)
-            right[whole, cols] = dot(weight, v).astype(BF16)
+            right[whole, cols] = dot(probs[m * HEADS + head], heads_of(2, head)).astype(BF16)
 
     def forward(i, load=False):
         at = slice(*spans[i])
@@ -300,20 +305,28 @@
         dctx[...] = dot_nt(left[OUT - 1, 0, at], w_out[...]).astype(BF16)
         hooks[1](m)
 
+        def heads_of(part, head):
+            start = part * width + head * HEAD_DIM
+            return proj[at, start : start + HEAD_DIM]
+
+        def keep(part, head, value):
+            start = columns_at[QKV] + part * width + head * HEAD_DIM
+            right[at, start : start + HEAD_DIM] = value.astype(BF16)
+
+        def grad_ctx(head):
+            return dctx[:, head * HEAD_DIM : (head + 1) * HEAD_DIM]
+
+        grad_scores = []
         for head in range(HEADS):
-            q, k, v = (proj[at, part * width + head * HEAD_DIM : part * width + (head + 1) * HEAD_DIM] for part in range(3))
-            grad_ctx = dctx[:, head * HEAD_DIM : (head + 1) * HEAD_DIM]
-            weight = probs[m * HEADS + head]
-            grad_weight = dot_nt(grad_ctx, v)
-            grad_v = dot_tn(weight, grad_ctx)
-            weight = weight.astype(F32)
+            weight = probs[m * HEADS + head].astype(F32)
+            grad_weight = dot_nt(grad_ctx(head), heads_of(2, head))
             total = jnp.sum(weight * grad_weight, axis=-1, keepdims=True)
-            grad_scores = (weight * (grad_weight - total)).astype(BF16)
-            grad_q = dot(grad_scores, k) * scale
-            grad_k = dot_tn(grad_scores, q) * scale
-            for part, value in enumerate((grad_q, grad_k, grad_v)):
-                start = columns_at[QKV] + part * width + head * HEAD_DIM
-                right[at, start : start + HEAD_DIM] = value.astype(BF16)
+            grad_scores.append((weight * (grad_weight - total)).astype(BF16))
+        for head in range(HEADS):
+            keep(2, head, dot_tn(probs[m * HEADS + head], grad_ctx(head)))
+        for head in range(HEADS):
+            keep(0, head, dot(grad_scores[head], heads_of(1, head)) * scale)
+            keep(1, head, dot_tn(grad_scores[head], heads_of(0, head)) * scale)
 
         twin_right_of(QKV, m).start()
         hooks[2](m)
@@ -341,20 +354,41 @@
         return send(parts.at[here, :, other_y], pair_beside.at[there], "pair_beside", here, beside, there)
 
     def in_of(p):
-        return send(acc.at[p % RING, pl.ds(1, 3)], pair_in.at[p % RING], "pair_in", p % RING, inner)
+        return send(acc.at[p % RING, pl.ds(1, 3)], pair_in.at[pl.ds(3 * (p % RING), 3)], "pair_in", p % RING, inner)
 
     def across_of(p):
-        return send(acc.at[p % RING, pl.ds(2, 2)], pair_across.at[p % RING], "pair_across", p % RING, across)
+        return send(acc.at[p % RING, 2], pair_across.at[p % RING], "pair_across", p % RING, across)
+
+    def far_of(p):
+        there = p % END_RING
+        return send(acc.at[p % RING, 3], pair_in.at[2 * there + 1], "pair_far", p % RING, far_end, there)
 
     def out_of(p):
-        return send(acc.at[p % RING, 0], pair_in.at[p % RING, 0], "pair_out", p % RING, end)
+        there = p % END_RING
+        return send(acc.at[p % RING, 0], pair_in.at[2 * there], "pair_out", p % RING, end, there)
+
+    def chunk_at(zz):
+        return pl.ds(pl.multiple_of((zz * PAIR + y) * chunk, chunk), chunk)
+
+    def vector_twin():
+        return send(vector, vectors.at[0], "vector", 0, twin)
+
+    def vector_beside():
+        return send(vector, vectors.at[1], "vector", 1, beside)
+
+    def vector_line(step):
+        return send(vector.at[:, chunk_at((z + step) % LINE)], vectors_line.at[step - 1], "vector", 1 + step, lined[step - 1])
 
     def strip_columns(p):
         return pl.ds(pl.multiple_of(p * strip, strip), strip)
 
     def fin_of(g):
         cols = pl.ds(pl.multiple_of(g * LEAVING * strip, LEAVING * strip), LEAVING * strip)
-        return send(fin.at[:, cols], out.at[core, :, cols], "fin", g, twin)
+        return send(fin.at[1, :, cols], out.at[core, :, cols], "fin", g, twin)
+
+    def kept_of(g):
+        cols = pl.ds(pl.multiple_of(g * LEAVING * strip, LEAVING * strip), LEAVING * strip)
+        return pltpu.make_async_copy(fin.at[0, :, cols], out.at[core, :, cols], sem["kept"].at[g])
 
     def add(target, *refs):
         total = target[...].astype(F32)
@@ -435,6 +469,10 @@
         def _():
             in_of(t + FIRST).start()
 
+        @pl.when((t < direct) & is_inner)
+        def _():
+            out_of(t).start()
+
     def across_y(t):
         @pl.when((t >= direct) & (t < strips))
         def _():
@@ -448,6 +486,10 @@
             def _():
                 in_of(t).start()
 
+            @pl.when(is_inner)
+            def _():
+                out_of(t).start()
+
             @pl.when(t + AHEAD < strips)
             def _():
                 @pl.when(t % STRIPS == STRIPS - 1)
@@ -462,43 +504,55 @@
         @pl.when((p >= 0) & (p < strips) & is_inner)
         def _():
             in_of(p).wait_recv()
-            add(acc.at[p % RING, pl.ds(2, 2)], pair_in.at[p % RING, pl.ds(1, 2)])
+            add(acc.at[p % RING, pl.ds(2, 2)], pair_in.at[pl.ds(3 * (p % RING) + 1, 2)])
+            far_of(p).start()
             across_of(p).start()
-            add(acc.at[p % RING, 1], pair_in.at[p % RING, 0])
-
-        q = t - 2 * LAG
-
-        @pl.when((q >= 0) & (q < strips) & is_inner)
-        def _():
-            across_of(q).wait_recv()
-            add(acc.at[q % RING, 0], pair_across.at[q % RING, 1])
-            out_of(q).start()
-            add(acc.at[q % RING, 1], pair_across.at[q % RING, 0])
-
-        r = t - 3 * LAG
+            add(acc.at[p % RING, 1], pair_in.at[3 * (p % RING)])
+
+        r = t - END_LAG
 
         @pl.when(r >= 0)
         def _():
             @pl.when(is_end)
             def _():
                 out_of(r).wait_recv()
-                add(acc.at[r % RING, 0], pair_in.at[r % RING, 0])
+                far_of(r).wait_recv()
                 in_of(r).wait_send()
+                finish(r, pair_in.at[2 * (r % END_RING)], pair_in.at[2 * (r % END_RING) + 1])
 
             @pl.when(is_inner)
             def _():
-                across_of(r).wait_send()
+                across_of(r).wait()
+                far_of(r).wait_send()
                 out_of(r).wait_send()
-
-            def block(which):
-                return acc[r % RING, own, pl.ds(pl.multiple_of(which * half_chunk, half_chunk), half_chunk)].astype(F32)
-
-            out[core, :, strip_columns(r)] = block(core)
-            fin[:, strip_columns(r)] = block(other_core)
-
-            @pl.when(r % LEAVING == LEAVING - 1)
-            def _():
-                fin_of(r // LEAVING).start()
+                finish(r, pair_across.at[r % RING])
+
+    def finish(r, *refs):
+        for slot, which in enumerate((core, other_core)):
+            here = pl.ds(pl.multiple_of(which * half_chunk, half_chunk), half_chunk)
+            total = acc[r % RING, own, here].astype(F32)
+            for ref in refs:
+                total = total + ref[here].astype(F32)
+            fin[slot, :, strip_columns(r)] = total
+
+        @pl.when(r % LEAVING == LEAVING - 1)
+        def _():
+            fin_of(r // LEAVING).start()
+            kept_of(r // LEAVING).start()
+
+    def vectors_step(t):
+        @pl.when(t == VECTORS[0])
+        def _():
+            vector_twin().wait()
+            vector[...] += vectors[0]
+            vector_beside().start()
+
+        @pl.when(t == VECTORS[1])
+        def _():
+            vector_beside().wait()
+            vector[...] += vectors[1]
+            for step in range(1, LINE):
+                vector_line(step).start()
 
     def proceed(low, high, parts_of_step):
         @pl.loop(low, high)
@@ -510,12 +564,13 @@
     def after_du(m):
         @pl.when((m == MICRO - 1) & leads)
         def _():
-            for i in range(2):
+            wait_for(UP)
+            form_up(0, 1)
+            start_strips(0, STRIPS)
+            for i in range(len(returns)):
                 gather_e(i)
-            wait_for(UP)
-            form_up(0, 2)
-            start_strips(0, 2 * STRIPS)
-            gather_e(2)
+            form_up(1, 2)
+            start_strips(STRIPS, 2 * STRIPS)
             form_down()
 
     def after_middle(m):
@@ -535,7 +590,7 @@
         load_rows.wait()
         attend(0, load=True)
 
-    pl.semaphore_wait(barrier, GROUP)
+    pl.semaphore_wait(barrier, len(peers))
 
     @pl.when(jnp.logical_not(leads))
     def _():
@@ -582,24 +637,13 @@
 
             @pl.when(leads & (m == 1))
             def _():
-                for i in (1, 2):
+                for i in range(1, len(returns)):
                     x_back(i).wait_recv()
                     spread(i)
 
             backward(m, (after_du, after_middle, after_heads))
 
-    def send_vector(step):
-        peer = (mine + step) % GROUP
-        start = pl.multiple_of((peer // CORES) * chunk, chunk)
-        return pltpu.make_async_remote_copy(
-            src_ref=vector.at[:, pl.ds(start, chunk)], dst_ref=vectors.at[mine],
-            send_sem=sem["vector_send"].at[step], recv_sem=sem["vector_recv"].at[mine],
-            device_id=(section, first + peer), device_id_type=MESH,
-        )
-
-    @pl.loop(1, GROUP)
-    def _(step):
-        send_vector(step).start()
+    vector_twin().start()
 
     @pl.when(jnp.logical_not(leads))
     def _():
@@ -609,27 +653,20 @@
         start_strips(0, AHEAD)
         for i in range(len(returns)):
             gather_e(i)
+        x_back(1).wait_send()
+        x_back(3).start()
         gather_act()
         form_down()
 
         proceed(0, BEFORE_LAST, (enter, relay))
 
-    proceed(BEFORE_LAST, strips + 3 * LAG, (enter, across_y, relay))
-
-    vector_total = vector[:, pl.ds(pl.multiple_of((mine // CORES) * chunk, chunk), chunk)]
-    for step in range(1, GROUP):
-        sender = (mine + step) % GROUP
-        pltpu.make_async_remote_copy(
-            src_ref=vector.at[:, pl.ds(0, chunk)], dst_ref=vectors.at[sender],
-            send_sem=sem["vector_send"].at[step], recv_sem=sem["vector_recv"].at[sender],
-            device_id=twin, device_id_type=MESH,
-        ).wait_recv()
-        vector_total = vector_total + vectors[sender]
-    vector_out[...] = vector_total
-
-    @pl.loop(1, GROUP)
-    def _(step):
-        send_vector(step).wait_send()
+    proceed(BEFORE_LAST, strips + END_LAG, (enter, relay, across_y, vectors_step))
+
+    total = vector[:, chunk_at(z)]
+    for step in range(1, LINE):
+        vector_line(step).wait()
+        total = total + vectors_line[step - 1]
+    vector_out[...] = total
 
     for m in range(MICRO):
         for which in (UP, OUT, QKV):
@@ -647,7 +684,7 @@
 
     @pl.when(jnp.logical_not(leads))
     def _():
-        for i in range(len(returns)):
+        for i in (0, 2, 3):
             x_back(i).wait_send()
 
     @pl.when(leads)
@@ -658,6 +695,7 @@
     @pl.loop(0, strips // LEAVING)
     def _(g):
         fin_of(g).wait()
+        kept_of(g).wait()
 
 
 def layers(tokens, cotangent, gains, biases, w_qkv, w_out, w_up, w_down):
@@ -692,21 +730,24 @@
         "vector": ((8, width), F32),
         "parts": ((AHEAD, LINE, PAIR, chunk, strip), BF16),
         "acc": ((RING, LINE, chunk, strip), BF16),
-        "fin": ((chunk // 2, columns // CORES), F32),
+        "fin": ((2, chunk // 2, columns // CORES), F32),
         "pair_beside": ((2 * AHEAD, LINE, chunk, strip), BF16),
-        "pair_in": ((RING, 3, chunk, strip), BF16),
-        "pair_across": ((RING, 2, chunk, strip), BF16),
-        "vectors": ((GROUP, 8, chunk), F32),
+        "pair_in": ((max(3 * RING, 2 * END_RING), chunk, strip), BF16),
+        "pair_across": ((RING, chunk, strip), BF16),
+        "vectors": ((2, 8, width), F32),
+        "vectors_line": ((LINE - 1, 8, chunk), F32),
     }
     exchanges = {
-        "x_forward": (3,), "x_back": (3,), "twin_left": (3, MICRO), "twin_right": (4, MICRO),
-        "act_beside": (2, MICRO), "e_half": (3, 3), "pair_in": (RING,), "pair_across": (RING,), "pair_out": (RING,),
-        "fin": (strips // LEAVING,), "vector": (GROUP,),
+        "x_forward": (3,), "x_back": (4,), "twin_left": (3, MICRO), "twin_right": (4, MICRO),
+        "act_beside": (2, MICRO), "e_half": (3, 4), "pair_in": (RING,), "pair_across": (RING,),
+        "fin": (strips // LEAVING,), "vector": (LINE + 1,),
     }
-    semaphores = {"fetch": dma((7,)), "store": dma((2, MICRO))}
+    semaphores = {"fetch": dma((7,)), "store": dma((2, MICRO)), "kept": dma((strips // LEAVING,))}
     for key, count in exchanges.items():
         semaphores[key + "_send"] = dma(count)
         semaphores[key + "_recv"] = dma(count)
+    for key in ("pair_out", "pair_far"):
+        semaphores[key + "_send"], semaphores[key + "_recv"] = dma((RING,)), dma((END_RING,))
     semaphores["pair_beside_send"], semaphores["pair_beside_recv"] = dma((AHEAD,)), dma((2 * AHEAD,))
     anywhere = pl.BlockSpec(memory_space=pl.ANY)
     in_vmem = pl.BlockSpec(memory_space=pltpu.VMEM)
@@ -719,7 +760,7 @@
             jax.ShapeDtypeStruct((8, chunk), F32),
         ),
         in_specs=[anywhere] * 2 + [in_vmem] * 2 + [anywhere] * 4,
-        out_specs=(anywhere, anywhere, in_vmem, in_vmem),
+        out_specs=(anywhere, anywhere, anywhere, in_vmem),
         scratch_shapes=[{key: pltpu.VMEM(*shape) for key, shape in shapes.items()}, semaphores],
         compiler_params=pltpu.CompilerParams(
             collective_id=1, has_side_effects=True, vmem_limit_bytes=64 * 2**20

time: 158 us -> 152 us (0.962)
  Pallas kernels: 157 us -> 151 us
    pallas_call x1, Pallas kernels: 154 us -> 147 us  [layers(): pl.pallas_call(layer_kernel, out_shape=(jax.ShapeDtypeStruct((all_rows, w...]
where the time goes in v4:
time: 152 us
  Pallas kernels  151 us (99%)
    pallas_call x1, Pallas kernels, layers(): pl.pallas_call(layer_kernel, out_shape=(jax.ShapeDtypeStruct((all_rows, w...  147 us
    pallas_call x1, Pallas kernels, results(): pl.pallas_call(results_kernel, out_shape=(jax.ShapeDtypeStruct(mixed.shap...  3.34 us

profile of v4, /device:TPU:0, one launch (start us, length us, event | category | flops | bytes accessed | tf_op | source)
XLA Modules:
  0.0 151.6 jit_solution(10350169871882161219)
XLA Ops:
  0.6 147.5 %relay_layers.1 = (bf16[480,1024]{1,0:T(8,128)(2,1)}, bf16[480,1024]{1,0:T(8,128)(2,1)}, f32[2,64,4096]{2,1,0:T(8,128)}, f32[8,128]{1,0:T(8,128)}) custom-call(bf16[480,1024]{1,0:T(8,128)(2,1)} %tokens_in.1, bf16[480,1024]{1,0:T(8,128)(2,1)} %cotangent_in.1, f32[2,1024]{1,0:T(2,128)} %bitcast.22, f32[2,1024]{1,0:T(2,128)} %bitcast.23, ...), custom_call_target="tpu_custom_call" | custom-call | tf_op jit(solution)/shard_map/relay_layers/pallas_call | solution.py:754
  148.1 3.3 %place_results.1 = (bf16[480,1024]{1,0:T(8,128)(2,1)}, bf16[480,1024]{1,0:T(8,128)(2,1)}, f32[64,2048]{1,0:T(8,128)}, f32[64,2048]{1,0:T(8,128)}, f32[64,1024]{1...) custom-call(bf16[480,1024]{1,0:T(8,128)(2,1)} %get-tuple-element.20.mixed_in, ...), custom_call_target="tpu_custom_call" | custom-call | tf_op jit(solution)/shard_map/place_results/pallas_call | solution.py:816

commit v5 on v4

--- a/solution.py
+++ b/solution.py
@@ -23,7 +23,7 @@
 BEFORE_HEADS, BEFORE_LAST = 4, 5
 RING = 8
 END_RING = 12
-VECTORS = 8, 22
+VECTORS = 8, 20, 28
 FIRST = 4
 LEAVING = 8
 MESH = pl.DeviceIdType.MESH
@@ -64,7 +64,7 @@
 
 
 def layer_kernel(
-    tokens_in, cotangent_in, gains, biases, w_qkv_in, w_out_in, w_up_in, w_down_in,
+    tokens_in, cotangent_in, gains_in, biases_in, w_qkv_in, w_out_in, w_up_in, w_down_in,
     mixed_out, grads_out, out, vector_out, buf, sem,
 ):
     h, e, e_other, result = buf["h"], buf["e"], buf["e_other"], buf["result"]
@@ -74,11 +74,12 @@
     probs, bias, dctx, vector = buf["probs"], buf["bias"], buf["dctx"], buf["vector"]
     parts, acc, fin = buf["parts"], buf["acc"], buf["fin"]
     pair_beside, pair_in, pair_across = buf["pair_beside"], buf["pair_in"], buf["pair_across"]
-    vectors, vectors_line = buf["vectors"], buf["vectors_line"]
+    vectors, vectors_line, vector_total = buf["vectors"], buf["vectors_line"], buf["vector_total"]
+    gains, biases = buf["gains"], buf["biases"]
 
     all_rows, width = h.shape
     rows = all_rows // MICRO
-    front = (rows // 2 + 15) // 16 * 16
+    front = rows // 32 * 16
     hidden = w_up.shape[1]
     chunk, half_chunk = acc.shape[2], acc.shape[2] // 2
     widths = (hidden, hidden, width, 3 * width)
@@ -129,26 +130,39 @@
         fetch(w_qkv_in.at[:, pl.ds(part * width, width)], w_qkv.at[:, pl.ds(part * width, width)], 3 + part)
         for part in range(3)
     ]
-    load_rows = fetch(tokens_in, h, 6)
+    load_rows = [fetch(tokens_in.at[at], h.at[at], 6 + i) for i, at in enumerate((pl.ds(0, front), pl.ds(front, all_rows - front)))]
+    load_cotangent = fetch(cotangent_in, e, 6)
+    load_norms = [fetch(gains_in, gains, 8), fetch(biases_in, biases, 9)]
 
     @pl.when(leads)
     def _():
-        load_rows.start()
+        load_rows[0].start()
 
     @pl.when(jnp.logical_not(leads))
     def _():
-        fetch(cotangent_in, e, 6).start()
-
+        load_cotangent.start()
+
+    for load in load_norms + loads_qkv[:2]:
+        load.start()
     barrier = pltpu.get_barrier_semaphore()
     lined = [device((z + step) % LINE, y, core) for step in range(1, LINE)]
     inner, end, across, far_end = (device(numbered(zz), y, core) for zz in (1, 0, 2, 3))
     peers = [partner, twin, beside] + lined
     for peer in peers:
         pl.semaphore_signal(barrier, inc=1, device_id=peer, device_id_type=MESH)
-    for load in loads_qkv:
-        load.start()
-    row_ids = lax.broadcasted_iota(jnp.int32, (rows, rows), 0)
-    col_ids = lax.broadcasted_iota(jnp.int32, (rows, rows), 1)
+    loads_qkv[2].start()
+
+    @pl.when(leads)
+    def _():
+        load_rows[1].start()
+
+    @pl.when(jnp.logical_not(leads))
+    def _():
+        for load in loads:
+            load.start()
+
+    row_ids = lax.broadcasted_iota(jnp.int32, (rows, 1), 0)
+    col_ids = lax.broadcasted_iota(jnp.int32, (1, rows), 1)
     seen = (row_ids // ITEM_LEN == col_ids // ITEM_LEN) & (col_ids <= row_ids)
     bias[...] = jnp.where(seen, 0.0, -1e30)
     vector[...] = jnp.zeros_like(vector)
@@ -163,7 +177,7 @@
         return send(result.at[at], h.at[at], "x_forward", i, partner)
 
     late = rows // 5
-    returns = ((0, rows), (rows, rows + front), (rows + front, 2 * rows - late), (2 * rows - late, 2 * rows))
+    returns = ((0, rows), (rows, 2 * rows - front), (2 * rows - front, 2 * rows - late), (2 * rows - late, 2 * rows))
 
     def returned(i):
         return pl.ds(returns[i][0], returns[i][1] - returns[i][0])
@@ -203,7 +217,7 @@
         return send(e_half.at[2, returned(i)], e_half.at[3, returned(i)], "e_half", (2, i), twin)
 
 
-    def attend(i, load=False):
+    def attend(i, load=False, first_section=False):
         low, high = spans[i]
         at, m = slice(low, high), low // rows
         whole = slice(m * rows, (m + 1) * rows)
@@ -213,8 +227,10 @@
             cols = slice(part * width, (part + 1) * width)
             if load:
                 loads_qkv[part].wait()
+            if load and first_section:
                 loads[part].start()
             proj[at, cols] = dot(left[QKV - 1, 0, at], w_qkv[:, cols]).astype(BF16)
+
         def heads_of(part, head):
             start = part * width + head * HEAD_DIM
             return proj[whole, start : start + HEAD_DIM]
@@ -286,13 +302,13 @@
     def backward(m, hooks):
         at = rows_of(m)
 
-        for part in range(2):
-            cols = slice(part * hidden // 2, (part + 1) * hidden // 2)
+        for part in (other_core, core):
+            start = pl.multiple_of(part * halves[UP], halves[UP])
+            cols = pl.ds(start, halves[UP])
             passed = dot_nt(e[at], w_down[cols])
-            slope = slopes[at, cols].astype(F32)
-            here = slice(columns_at[UP] + cols.start, columns_at[UP] + cols.stop)
-            right[at, here] = (passed * slope).astype(BF16)
-        twin_right_of(UP, m).start()
+            right[at, pl.ds(columns_at[UP] + start, halves[UP])] = (passed * slopes[at, cols].astype(F32)).astype(BF16)
+            if part is other_core:
+                twin_right_of(UP, m).start()
 
         hooks[0](m)
         grad = dot_nt(right[at, columns_at[UP] : columns_at[UP] + hidden], w_up[...])
@@ -370,6 +386,8 @@
     def chunk_at(zz):
         return pl.ds(pl.multiple_of((zz * PAIR + y) * chunk, chunk), chunk)
 
+    vector_store = pltpu.make_async_copy(vector_total, vector_out, sem["vector_store"].at[0])
+
     def vector_twin():
         return send(vector, vectors.at[0], "vector", 0, twin)
 
@@ -554,6 +572,15 @@
             for step in range(1, LINE):
                 vector_line(step).start()
 
+        @pl.when(t == VECTORS[2])
+        def _():
+            total = vector[:, chunk_at(z)]
+            for step in range(1, LINE):
+                vector_line(step).wait()
+                total = total + vectors_line[step - 1]
+            vector_total[...] = total
+            vector_store.start()
+
     def proceed(low, high, parts_of_step):
         @pl.loop(low, high)
         def _(t):
@@ -587,20 +614,26 @@
 
     @pl.when(leads)
     def _():
-        load_rows.wait()
-        attend(0, load=True)
+        for load in load_rows[:1] + load_norms:
+            load.wait()
+        attend(0, load=True, first_section=True)
 
     pl.semaphore_wait(barrier, len(peers))
 
     @pl.when(jnp.logical_not(leads))
     def _():
-        load_rows.wait()
+        for load in [load_cotangent] + load_norms:
+            load.wait()
         for i in range(len(returns)):
             spread(i)
         x_forward(0).wait_recv()
         attend(0, load=True)
 
     forward(0, load=True)
+
+    @pl.when(leads)
+    def _():
+        load_rows[1].wait()
 
     @pl.when(jnp.logical_not(leads))
     def _():
@@ -662,12 +695,7 @@
 
     proceed(BEFORE_LAST, strips + END_LAG, (enter, relay, across_y, vectors_step))
 
-    total = vector[:, chunk_at(z)]
-    for step in range(1, LINE):
-        vector_line(step).wait()
-        total = total + vectors_line[step - 1]
-    vector_out[...] = total
-
+    vector_store.wait()
     for m in range(MICRO):
         for which in (UP, OUT, QKV):
             twin_left(which, m).wait_send()
@@ -736,13 +764,16 @@
         "pair_across": ((RING, chunk, strip), BF16),
         "vectors": ((2, 8, width), F32),
         "vectors_line": ((LINE - 1, 8, chunk), F32),
+        "vector_total": ((8, chunk), F32),
+        "gains": (gains.shape, F32),
+        "biases": (biases.shape, F32),
     }
     exchanges = {
         "x_forward": (3,), "x_back": (4,), "twin_left": (3, MICRO), "twin_right": (4, MICRO),
         "act_beside": (2, MICRO), "e_half": (3, 4), "pair_in": (RING,), "pair_across": (RING,),
         "fin": (strips // LEAVING,), "vector": (LINE + 1,),
     }
-    semaphores = {"fetch": dma((7,)), "store": dma((2, MICRO)), "kept": dma((strips // LEAVING,))}
+    semaphores = {"fetch": dma((10,)), "vector_store": dma((1,)), "store": dma((2, MICRO)), "kept": dma((strips // LEAVING,))}
     for key, count in exchanges.items():
         semaphores[key + "_send"] = dma(count)
         semaphores[key + "_recv"] = dma(count)
@@ -750,7 +781,6 @@
         semaphores[key + "_send"], semaphores[key + "_recv"] = dma((RING,)), dma((END_RING,))
     semaphores["pair_beside_send"], semaphores["pair_beside_recv"] = dma((AHEAD,)), dma((2 * AHEAD,))
     anywhere = pl.BlockSpec(memory_space=pl.ANY)
-    in_vmem = pl.BlockSpec(memory_space=pltpu.VMEM)
     return pl.pallas_call(
         layer_kernel,
         out_shape=(
@@ -759,8 +789,8 @@
             jax.ShapeDtypeStruct((CORES, chunk // 2, columns // CORES), F32),
             jax.ShapeDtypeStruct((8, chunk), F32),
         ),
-        in_specs=[anywhere] * 2 + [in_vmem] * 2 + [anywhere] * 4,
-        out_specs=(anywhere, anywhere, anywhere, in_vmem),
+        in_specs=[anywhere] * 8,
+        out_specs=(anywhere,) * 4,
         scratch_shapes=[{key: pltpu.VMEM(*shape) for key, shape in shapes.items()}, semaphores],
         compiler_params=pltpu.CompilerParams(
             collective_id=1, has_side_effects=True, vmem_limit_bytes=64 * 2**20

time: 152 us -> 151 us (level)
  no operation moved by 1% of the time
where the time goes in v5:
time: 151 us; the launch traced here: 150 us
  Pallas kernels  150 us (99%)
    pallas_call x1, Pallas kernels, layers(): pl.pallas_call(layer_kernel, out_shape=(jax.ShapeDtypeStruct((all_rows, w...  146 us
    pallas_call x1, Pallas kernels, results(): pl.pallas_call(results_kernel, out_shape=(jax.ShapeDtypeStruct(mixed.shap...  3.34 us

profile of v5, /device:TPU:0, one launch (start us, length us, event | category | flops | bytes accessed | tf_op | source)
XLA Modules:
  0.0 150.5 jit_solution(4056324517207434667)
XLA Ops:
  0.6 146.3 %relay_layers.1 = (bf16[480,1024]{1,0:T(8,128)(2,1)}, bf16[480,1024]{1,0:T(8,128)(2,1)}, f32[2,64,4096]{2,1,0:T(8,128)}, f32[8,128]{1,0:T(8,128)}) custom-call(bf16[480,1024]{1,0:T(8,128)(2,1)} %tokens_in.1, bf16[480,1024]{1,0:T(8,128)(2,1)} %cotangent_in.1, f32[2,1024]{1,0:T(2,128)} %bitcast.22, f32[2,1024]{1,0:T(2,128)} %bitcast.23, ...), custom_call_target="tpu_custom_call" | custom-call | tf_op jit(solution)/shard_map/relay_layers/pallas_call | solution.py:784
  147.0 3.3 %place_results.1 = (bf16[480,1024]{1,0:T(8,128)(2,1)}, bf16[480,1024]{1,0:T(8,128)(2,1)}, f32[64,2048]{1,0:T(8,128)}, f32[64,2048]{1,0:T(8,128)}, f32[64,1024]{1...) custom-call(bf16[480,1024]{1,0:T(8,128)(2,1)} %get-tuple-element.20.mixed_in, ...), custom_call_target="tpu_custom_call" | custom-call | tf_op jit(solution)/shard_map/place_results/pallas_call | solution.py:846

commit v6 on v5

--- a/solution.py
+++ b/solution.py
@@ -17,13 +17,14 @@
 GROUP = LINE * PAIR * CORES
 PANEL = 256
 STRIPS = 2
-AHEAD = 10
+AHEAD = 8
 LAG = 2
 END_LAG = 5
-BEFORE_HEADS, BEFORE_LAST = 4, 5
+BEFORE_HEADS, BEFORE_LAST = 4, 6
 RING = 8
 END_RING = 12
 VECTORS = 8, 20, 28
+SPARE, ACROSS, BACK = 12, 12, 20
 FIRST = 4
 LEAVING = 8
 MESH = pl.DeviceIdType.MESH
@@ -76,6 +77,7 @@
     pair_beside, pair_in, pair_across = buf["pair_beside"], buf["pair_in"], buf["pair_across"]
     vectors, vectors_line, vector_total = buf["vectors"], buf["vectors_line"], buf["vector_total"]
     gains, biases = buf["gains"], buf["biases"]
+    spare_parts, spare_in, spare_across = buf["spare_parts"], buf["spare_in"], buf["spare_across"]
 
     all_rows, width = h.shape
     rows = all_rows // MICRO
@@ -369,6 +371,20 @@
         here, there = i % AHEAD, i % (2 * AHEAD)
         return send(parts.at[here, :, other_y], pair_beside.at[there], "pair_beside", here, beside, there)
 
+    def spare_out(part):
+        return send(spare_parts.at[part, :, other_y], spare_in.at[part], "spare", part, partner)
+
+    def spare_beside(part, d):
+        return send(spare_in.at[part, d], spare_across.at[part, d], "spare_across", (part, d), beside)
+
+    def spare_back(part):
+        return send(spare_across.at[part], spare_in.at[part], "spare", part, partner)
+
+    def each_spare(act):
+        for part in range(STRIPS):
+            for d in range(LINE):
+                act(spare_beside(part, d))
+
     def in_of(p):
         return send(acc.at[p % RING, pl.ds(1, 3)], pair_in.at[pl.ds(3 * (p % RING), 3)], "pair_in", p % RING, inner)
 
@@ -430,12 +446,13 @@
             twin_left(which, m).wait_recv()
             twin_right_of(which, m).wait_recv()
 
-    def form(p):
-        which = 0
-        for i in (OUT, QKV):
+    def form(p, spare=False):
+        which = QKV - 1 if spare else 0
+        for i in () if spare else (OUT, QKV):
             which = which + (p >= starts[i]).astype(jnp.int32)
-
-            @pl.when(p == starts[i])
+            due = p == starts[i] if i == OUT else (p == starts[i]) & jnp.logical_not(leads)
+
+            @pl.when(due)
             def _(i=i):
                 wait_for(i)
 
@@ -444,7 +461,10 @@
         for part in range(STRIPS):
             for zz in range(LINE):
                 here = total[zz, :, :, part * strip : (part + 1) * strip]
-                parts[(p * STRIPS + part - direct) % AHEAD, numbered(zz)] = here
+                if spare:
+                    spare_parts[part, numbered(zz)] = here
+                else:
+                    parts[(p * STRIPS + part - direct) % AHEAD, numbered(zz)] = here
 
     def form_up(low, high):
         @pl.loop(starts[UP] + low, starts[UP] + high)
@@ -492,29 +512,51 @@
             out_of(t).start()
 
     def across_y(t):
-        @pl.when((t >= direct) & (t < strips))
+        def enter_line(mine_of, theirs_of):
+            for d in range(LINE):
+                acc[t % RING, d] = (mine_of(d).astype(F32) + theirs_of(d).astype(F32)).astype(BF16)
+
+            @pl.when(is_end)
+            def _():
+                in_of(t).start()
+
+            @pl.when(is_inner)
+            def _():
+                out_of(t).start()
+
+        spared = leads & (t // STRIPS == SPARE)
+
+        @pl.when((t >= direct) & (t < strips) & jnp.logical_not(spared))
         def _():
             i = t - direct
             beside_of(t).wait()
-            for d in range(LINE):
-                total = parts[i % AHEAD, d, y].astype(F32) + pair_beside[i % (2 * AHEAD), d].astype(F32)
-                acc[t % RING, d] = total.astype(BF16)
-
-            @pl.when(is_end)
-            def _():
-                in_of(t).start()
-
-            @pl.when(is_inner)
-            def _():
-                out_of(t).start()
-
-            @pl.when(t + AHEAD < strips)
-            def _():
-                @pl.when(t % STRIPS == STRIPS - 1)
-                def _():
-                    form((t + AHEAD) // STRIPS)
-                    for part in range(STRIPS):
-                        beside_of(t + AHEAD - STRIPS + 1 + part).start()
+            enter_line(lambda d: parts[i % AHEAD, d, y], lambda d: pair_beside[i % (2 * AHEAD), d])
+
+            panel = (t + AHEAD) // STRIPS
+
+            @pl.when((t + AHEAD < strips) & (t % STRIPS == STRIPS - 1) & jnp.logical_not(leads & (panel == SPARE)))
+            def _():
+                form(panel)
+                for part in range(STRIPS):
+                    beside_of(t + AHEAD - STRIPS + 1 + part).start()
+
+        @pl.when(spared)
+        def _():
+            part = t % STRIPS
+            spare_back(part).wait_recv()
+            enter_line(lambda d: spare_parts[part, d, y], lambda d: spare_in[part, d])
+
+        @pl.when((t == ACROSS) & jnp.logical_not(leads))
+        def _():
+            for part in range(STRIPS):
+                spare_out(part).wait_recv()
+            each_spare(lambda message: message.start())
+
+        @pl.when((t == BACK) & jnp.logical_not(leads))
+        def _():
+            each_spare(lambda message: message.wait_recv())
+            for part in range(STRIPS):
+                spare_back(part).start()
 
     def relay(t):
         p = t - LAG
@@ -677,6 +719,13 @@
             backward(m, (after_du, after_middle, after_heads))
 
     vector_twin().start()
+
+    @pl.when(leads)
+    def _():
+        wait_for(QKV)
+        form(SPARE, spare=True)
+        for part in range(STRIPS):
+            spare_out(part).start()
 
     @pl.when(jnp.logical_not(leads))
     def _():
@@ -696,6 +745,13 @@
     proceed(BEFORE_LAST, strips + END_LAG, (enter, relay, across_y, vectors_step))
 
     vector_store.wait()
+    for part in range(STRIPS):
+        spare_out(part).wait_send()
+
+    @pl.when(jnp.logical_not(leads))
+    def _():
+        each_spare(lambda message: message.wait_send())
+
     for m in range(MICRO):
         for which in (UP, OUT, QKV):
             twin_left(which, m).wait_send()
@@ -762,6 +818,9 @@
         "pair_beside": ((2 * AHEAD, LINE, chunk, strip), BF16),
         "pair_in": ((max(3 * RING, 2 * END_RING), chunk, strip), BF16),
         "pair_across": ((RING, chunk, strip), BF16),
+        "spare_parts": ((STRIPS, LINE, PAIR, chunk, strip), BF16),
+        "spare_in": ((STRIPS, LINE, chunk, strip), BF16),
+        "spare_across": ((STRIPS, LINE, chunk, strip), BF16),
         "vectors": ((2, 8, width), F32),
         "vectors_line": ((LINE - 1, 8, chunk), F32),
         "vector_total": ((8, chunk), F32),
@@ -771,7 +830,7 @@
     exchanges = {
         "x_forward": (3,), "x_back": (4,), "twin_left": (3, MICRO), "twin_right": (4, MICRO),
         "act_beside": (2, MICRO), "e_half": (3, 4), "pair_in": (RING,), "pair_across": (RING,),
-        "fin": (strips // LEAVING,), "vector": (LINE + 1,),
+        "fin": (strips // LEAVING,), "spare": (STRIPS,), "spare_across": (STRIPS, LINE), "vector": (LINE + 1,),
     }
     semaphores = {"fetch": dma((10,)), "vector_store": dma((1,)), "store": dma((2, MICRO)), "kept": dma((strips // LEAVING,))}
     for key, count in exchanges.items():

time: 151 us -> 148 us (0.980)
  Pallas kernels: 150 us -> 147 us
    pallas_call x1, Pallas kernels: 146 us -> 144 us  [layers(): pl.pallas_call(layer_kernel, out_shape=(jax.ShapeDtypeStruct((all_rows, w...]
where the time goes in v6:
time: 148 us
  Pallas kernels  147 us (99%)
    pallas_call x1, Pallas kernels, layers(): pl.pallas_call(layer_kernel, out_shape=(jax.ShapeDtypeStruct((all_rows, w...  144 us
    pallas_call x1, Pallas kernels, results(): pl.pallas_call(results_kernel, out_shape=(jax.ShapeDtypeStruct(mixed.shap...  3.34 us

profile of v6, /device:TPU:0, one launch (start us, length us, event | category | flops | bytes accessed | tf_op | source)
XLA Modules:
  0.0 148.1 jit_solution(2979526114749784379)
XLA Ops:
  0.6 144.0 %relay_layers.1 = (bf16[480,1024]{1,0:T(8,128)(2,1)}, bf16[480,1024]{1,0:T(8,128)(2,1)}, f32[2,64,4096]{2,1,0:T(8,128)}, f32[8,128]{1,0:T(8,128)}) custom-call(bf16[480,1024]{1,0:T(8,128)(2,1)} %tokens_in.1, bf16[480,1024]{1,0:T(8,128)(2,1)} %cotangent_in.1, f32[2,1024]{1,0:T(2,128)} %bitcast.22, f32[2,1024]{1,0:T(2,128)} %bitcast.23, ...), custom_call_target="tpu_custom_call" | custom-call | tf_op jit(solution)/shard_map/relay_layers/pallas_call | solution.py:843
  144.6 3.3 %place_results.1 = (bf16[480,1024]{1,0:T(8,128)(2,1)}, bf16[480,1024]{1,0:T(8,128)(2,1)}, f32[64,2048]{1,0:T(8,128)}, f32[64,2048]{1,0:T(8,128)}, f32[64,1024]{1...) custom-call(bf16[480,1024]{1,0:T(8,128)(2,1)} %get-tuple-element.20.mixed_in, ...), custom_call_target="tpu_custom_call" | custom-call | tf_op jit(solution)/shard_map/place_results/pallas_call | solution.py:905

commit v7 on v6

--- a/solution.py
+++ b/solution.py
@@ -225,7 +225,7 @@
         whole = slice(m * rows, (m + 1) * rows)
         unit, unused = normalized(h[at].astype(F32))
         left[QKV - 1, 0, at] = (unit * gains[0:1] + biases[0:1]).astype(BF16)
-        for part in range(3):
+        def project(part):
             cols = slice(part * width, (part + 1) * width)
             if load:
                 loads_qkv[part].wait()
@@ -233,6 +233,9 @@
                 loads[part].start()
             proj[at, cols] = dot(left[QKV - 1, 0, at], w_qkv[:, cols]).astype(BF16)
 
+        project(0)
+        project(1)
+
         def heads_of(part, head):
             start = part * width + head * HEAD_DIM
             return proj[whole, start : start + HEAD_DIM]
@@ -241,6 +244,7 @@
             scores = dot_nt(heads_of(0, head), heads_of(1, head)) * scale + bias[...]
             weight = jnp.exp(scores - jnp.max(scores, axis=-1, keepdims=True))
             probs[m * HEADS + head] = (weight / jnp.sum(weight, axis=-1, keepdims=True)).astype(BF16)
+        project(2)
         for head in range(HEADS):
             cols = slice(columns_at[OUT] + head * HEAD_DIM, columns_at[OUT] + (head + 1) * HEAD_DIM)
             right[whole, cols] = dot(probs[m * HEADS + head], heads_of(2, head)).astype(BF16)
@@ -272,11 +276,11 @@
             x_forward(i).start()
 
     def share(m):
-        mixed_store(m).start()
+        twin_left(UP, m).start()
         twin_right_of(DOWN, m).start()
         twin_right_of(OUT, m).start()
         twin_left(QKV, m).start()
-        twin_left(UP, m).start()
+        mixed_store(m).start()
 
     def gather_act():
         cols = pl.ds(pl.multiple_of(core * halves[DOWN], 128), halves[DOWN])
@@ -683,7 +687,10 @@
 
     attend(1)
     forward(1)
-    share(0)
+
+    @pl.when(leads)
+    def _():
+        share(0)
 
     @pl.loop(0, MICRO + 1)
     def _(step):
@@ -695,10 +702,10 @@
 
             attend(2)
             forward(2)
-            share(1)
 
             @pl.when(leads)
             def _():
+                share(1)
                 gather_act()
 
         @pl.when(step != section)
@@ -729,16 +736,20 @@
 
     @pl.when(jnp.logical_not(leads))
     def _():
-        wait_for(UP)
-        form_up(0, AHEAD // STRIPS)
-        x_back(2).start()
-        start_strips(0, AHEAD)
+        for m in range(MICRO):
+            share(m)
         for i in range(len(returns)):
             gather_e(i)
+        x_back(2).start()
+        wait_for(UP)
+        form_up(0, 2)
+        start_strips(0, 2 * STRIPS)
         x_back(1).wait_send()
         x_back(3).start()
         gather_act()
         form_down()
+        form_up(2, AHEAD // STRIPS)
+        start_strips(2 * STRIPS, AHEAD)
 
         proceed(0, BEFORE_LAST, (enter, relay))
 

time: 148 us -> 148 us (level)
  no operation moved by 1% of the time
where the time goes in v7:
time: 148 us
  Pallas kernels  147 us (99%)
    pallas_call x1, Pallas kernels, layers(): pl.pallas_call(layer_kernel, out_shape=(jax.ShapeDtypeStruct((all_rows, w...  144 us
    pallas_call x1, Pallas kernels, results(): pl.pallas_call(results_kernel, out_shape=(jax.ShapeDtypeStruct(mixed.shap...  3.34 us

profile of v7, /device:TPU:0, one launch (start us, length us, event | category | flops | bytes accessed | tf_op | source)
XLA Modules:
  0.0 147.7 jit_solution(8041430193690085736)
XLA Ops:
  0.6 143.6 %relay_layers.1 = (bf16[480,1024]{1,0:T(8,128)(2,1)}, bf16[480,1024]{1,0:T(8,128)(2,1)}, f32[2,64,4096]{2,1,0:T(8,128)}, f32[8,128]{1,0:T(8,128)}) custom-call(bf16[480,1024]{1,0:T(8,128)(2,1)} %tokens_in.1, bf16[480,1024]{1,0:T(8,128)(2,1)} %cotangent_in.1, f32[2,1024]{1,0:T(2,128)} %bitcast.22, f32[2,1024]{1,0:T(2,128)} %bitcast.23, ...), custom_call_target="tpu_custom_call" | custom-call | tf_op jit(solution)/shard_map/relay_layers/pallas_call | solution.py:854
  144.2 3.3 %place_results.1 = (bf16[480,1024]{1,0:T(8,128)(2,1)}, bf16[480,1024]{1,0:T(8,128)(2,1)}, f32[64,2048]{1,0:T(8,128)}, f32[64,2048]{1,0:T(8,128)}, f32[64,1024]{1...) custom-call(bf16[480,1024]{1,0:T(8,128)(2,1)} %get-tuple-element.20.mixed_in, ...), custom_call_target="tpu_custom_call" | custom-call | tf_op jit(solution)/shard_map/place_results/pallas_call | solution.py:916

commit v8 on v7

--- a/solution.py
+++ b/solution.py
@@ -880,18 +880,20 @@
         started[-1].start()
         return started[-1]
 
-    fetches = [copy(block_in.at[core], block.at[core]) for core in range(CORES)]
-    fetches.append(copy(vectors_in, vectors))
-    fetches += [copy(ref, rows.at[i]) for i, ref in enumerate((mixed_in, grads_in))]
+    row_fetches = [copy(ref, rows.at[i]) for i, ref in enumerate((mixed_in, grads_in))]
+    fetches = [copy(vectors_in, vectors)] + [copy(block_in.at[core], block.at[core]) for core in range(CORES)]
     stores = []
+    for i, ref in enumerate((mixed, grads)):
+        row_fetches[i].wait()
+        stores.append(copy(rows.at[i], ref))
     for core in range(CORES):
-        fetches[core].wait()
+        fetches[1 + core].wait()
         offset = 0
         for ref in (down, up, out, qkv):
             half = ref.shape[1] // CORES
             stores.append(copy(block.at[core, :, pl.ds(offset, half)], ref.at[:, pl.ds(core * half, half)]))
             offset += half
-    fetches[CORES].wait()
+    fetches[0].wait()
     share = gains.shape[1]
     mine = lax.axis_index("dp") % CORES
     for core in range(CORES):
@@ -902,9 +904,6 @@
             shares[1] = vectors[2:4, here]
 
     stores += [copy(shares.at[i], ref) for i, ref in enumerate((gains, biases))]
-    for i, ref in enumerate((mixed, grads)):
-        fetches[CORES + 1 + i].wait()
-        stores.append(copy(rows.at[i], ref))
     for store in stores:
         store.wait()
 

time: 148 us -> 148 us (level)
  no operation moved by 1% of the time
where the time goes in v8:
time: 148 us
  Pallas kernels  147 us (99%)
    pallas_call x1, Pallas kernels, layers(): pl.pallas_call(layer_kernel, out_shape=(jax.ShapeDtypeStruct((all_rows, w...  144 us
    pallas_call x1, Pallas kernels, results(): pl.pallas_call(results_kernel, out_shape=(jax.ShapeDtypeStruct(mixed.shap...  3.31 us

profile of v8, /device:TPU:0, one launch (start us, length us, event | category | flops | bytes accessed | tf_op | source)
XLA Modules:
  0.0 147.7 jit_solution(1427858370082870544)
XLA Ops:
  0.6 143.6 %relay_layers.1 = (bf16[480,1024]{1,0:T(8,128)(2,1)}, bf16[480,1024]{1,0:T(8,128)(2,1)}, f32[2,64,4096]{2,1,0:T(8,128)}, f32[8,128]{1,0:T(8,128)}) custom-call(bf16[480,1024]{1,0:T(8,128)(2,1)} %tokens_in.1, bf16[480,1024]{1,0:T(8,128)(2,1)} %cotangent_in.1, f32[2,1024]{1,0:T(2,128)} %bitcast.22, f32[2,1024]{1,0:T(2,128)} %bitcast.23, ...), custom_call_target="tpu_custom_call" | custom-call | tf_op jit(solution)/shard_map/relay_layers/pallas_call | solution.py:854
  144.2 3.3 %place_results.1 = (bf16[480,1024]{1,0:T(8,128)(2,1)}, bf16[480,1024]{1,0:T(8,128)(2,1)}, f32[64,2048]{1,0:T(8,128)}, f32[64,2048]{1,0:T(8,128)}, f32[64,1024]{1...) custom-call(bf16[480,1024]{1,0:T(8,128)(2,1)} %get-tuple-element.20.mixed_in, ...), custom_call_target="tpu_custom_call" | custom-call | tf_op jit(solution)/shard_map/place_results/pallas_call | solution.py:915
